TPU v7x, 512 devices: a whole 4x8x8 slice. The times are simulated.
512 devices in a mesh: dp: 32 (over y, z_lo, core), mp: 16 (over x, z_hi).
Axes of the slice: x: 4, y: 8, z: 8 (z_hi: 4, z_lo: 2; z = z_hi * 2 + z_lo), core: 2. Of those that a mesh axis runs over, the one named last changes fastest.
Arguments:
- activations: bfloat16 [32768, 4096], P('dp', 'mp'), may hold values from -6 to 6
- output_gradient_rows: bfloat16 [32768, 4096], P('dp', 'mp'), may hold values from -6 to 6
- adapter_up_matrix: bfloat16 [4096, 128], P('mp'), may hold values from -0.09375 to 0.09375
- rank_factor_signs: int32 [64, 128], replicated, may hold values from 0 to 65535
- feature_factor_signs: int32 [64, 4096], P(None, 'mp'), may hold values from 0 to 65535
- lengths: int32 [1024], P('dp'), may hold values from 1 to 32, 16384 in all
Outputs:
- sketches: bfloat16 [1024, 1024], P(('dp', 'mp'))
- cosines: float32 [1024, 32, 32], P('dp', None, 'mp')
Inputs may be any that keep to these rules, and one draw needn't show every extreme that they name: `lengths`: every example has at least one live token and some example fills all 32 slots.
All inputs are finite; a program needn't handle non-finite values. No bound on the sum of `lengths` on one device may be relied on, other than what follows from the above.
Results may differ from a plain program's by a relative error of at most 0.004.
Values may be sent and summed in bfloat16 or wider, within the bound.
A program may use at most 64 MiB of HBM per device.

v0:
```python
import jax
import jax.numpy as jnp
from jax import lax
from jax.sharding import PartitionSpec as P


def from_behind(value, axis, steps):
    count = lax.axis_size(axis)
    pairs = [(source, (source + steps) % count) for source in range(count)]
    return lax.ppermute(value, axis, pairs)


def unpack_signs(packed):
    offsets = jnp.arange(16, dtype=jnp.int32)
    bit_values = jnp.bitwise_and(jnp.right_shift(packed[:, None, :], offsets[None, :, None]), 1)
    return (2 * bit_values - 1).reshape(packed.shape[0] * 16, packed.shape[1]).astype(jnp.bfloat16)


def unit_rows(raw_sum):
    scaled = raw_sum * lax.rsqrt(jnp.mean(raw_sum * raw_sum, axis=1, keepdims=True) + 1e-06)
    return scaled.astype(jnp.bfloat16)


def project_rank(rank_values, sign_rank):
    return lax.dot_general(
        rank_values,
        sign_rank,
        (((1,), (1,)), ((), ())),
        precision=lax.Precision.HIGHEST,
        preferred_element_type=jnp.float32,
    )


def per_device(
    activations,
    output_gradient_rows,
    adapter_up_matrix,
    rank_factor_signs,
    feature_factor_signs,
    lengths,
):
    ex_dev = lengths.shape[0]
    tok_rows = activations.shape[0]
    seq_len = tok_rows // ex_dev
    sketch_width = 16 * rank_factor_signs.shape[0]
    positions = lax.broadcasted_iota(jnp.int32, (ex_dev, seq_len), 1)
    active_mask = (positions < lengths[:, None]).astype(jnp.float32).reshape(tok_rows, 1)
    rank_portion = (
        jnp.dot(output_gradient_rows, adapter_up_matrix, preferred_element_type=jnp.float32)
        * active_mask
    )
    sign_rank = unpack_signs(rank_factor_signs).astype(jnp.float32)
    rank_full = lax.psum(rank_portion, "mp")
    left_proj = project_rank(rank_full, sign_rank)
    sign_feat = unpack_signs(feature_factor_signs)
    right_proj = lax.dot_general(
        activations, sign_feat, (((1,), (1,)), ((), ())), preferred_element_type=jnp.float32
    )
    partial_value = (left_proj * right_proj).reshape(ex_dev, seq_len, sketch_width).sum(axis=1)
    own_count = ex_dev // lax.axis_size("mp")
    own_block = unit_rows(lax.psum_scatter(partial_value, "mp", scatter_dimension=0, tiled=True))
    rows_unit = lax.all_gather(own_block, "mp", axis=0, tiled=True)

    def cos_tile(other_block):
        product = lax.dot_general(
            rows_unit, other_block, (((1,), (1,)), ((), ())), preferred_element_type=jnp.float32
        )
        return (product / sketch_width)[:, None, :]

    loop_size = lax.axis_size("dp")
    my_index = lax.axis_index("dp")
    zero_index = jnp.int32(0)
    cos_table = jnp.zeros((ex_dev, loop_size, own_count), jnp.float32)
    cos_table = lax.dynamic_update_slice(
        cos_table, cos_tile(own_block), (zero_index, my_index, zero_index)
    )

    def advance_one(turn_index, carry):
        travelling, table_now = carry
        travelling = from_behind(travelling, "dp", 1)
        source = (my_index - turn_index) % loop_size
        table_now = lax.dynamic_update_slice(
            table_now, cos_tile(travelling), (zero_index, source, zero_index)
        )
        return (travelling, table_now)

    travelling, cos_table = lax.fori_loop(1, loop_size, advance_one, (own_block, cos_table))
    return (own_block, cos_table)


def solution(mesh):
    return jax.shard_map(
        per_device,
        mesh=mesh,
        in_specs=(P("dp", "mp"), P("dp", "mp"), P("mp", None), P(), P(None, "mp"), P("dp")),
        out_specs=(P(("dp", "mp"), None), P("dp", None, "mp")),
        check_vma=False,
    )
```

profile of v0, /device:TPU:1, one launch (start us, length us, event | category | flops | bytes accessed | tf_op | source)
XLA Modules:
  0.0 634.1 jit_solution(10592861999988257220)
XLA Ops:
  8.2 2.0 convolution_multiply_fusion.1
  12.4 167.0 %all-reduce.4.cloned.1.call-done = f32[1024,128]{1,0:T(8,128)} async-done(((f32[1024,128]{1,0:T(8,128)}), f32[1024,128]{1,0:T(8,128)}) %all-reduce.4.cloned.1.call-update) | async-done | bytes 524304 | tf_op jit(solution)/shard_map/psum | solution.py:53
  179.4 2.8 fusion.13
  185.7 166.7 %all-reduce.6.cloned.1.call-done = f32[32,1024]{1,0:T(8,128)} async-done(((f32[32,1024]{1,0:T(8,128)}), f32[32,1024]{1,0:T(8,128)}) %all-reduce.6.cloned.1.call-update) | async-done | bytes 131088
  354.2 35.5 %all-gather = bf16[16,2,1024]{2,1,0:T(2,128)(2,1)S(1)} all-gather(bf16[1,2,1024]{2,1,0:T(2,128)(2,1)S(1)} %fusion.24), channel_id=1, replica_groups=mesh['dp'=32,'mp'=16] {'mp'}, dimensions={0}, use_global_device_ids=true | all-gather | bytes 69632 | tf_op jit(solution)/shard_map/all_gather | solution.py:62
  390.7 235.8 %while.17 = (s32[]{:T(128)}, bf16[2,1024]{1,0:T(2,128)(2,1)S(1)}, f32[32,32,2]{0,2,1:T(2,128)S(1)}, bf16[32,1024]{1,0:T(8,128)(2,1)S(1)}, s32[]{:T(128)}, /*index=5*/s32[]{:T(128)}, s32[]{:T(128)}, s32[]{:T(128)}, s32[]{:T(128)}) while((s32[]{:T(128)}, bf16[2,1024]{1,0:T(2,128)(2,1)S(1)}, f32[32,32,2]{0,2,1:T(2,128)S(1)}, ...), condition=%wide.region_5.6_spmd, body=%wide.region_4.5_spmd.sunk | while | flops 131153 | bytes 95524 | solution.py:87
  390.7 20.2 %collective-permute-start = (bf16[2,1024]{1,0:T(2,128)(2,1)S(1)}, bf16[2,1024]{1,0:T(2,128)(2,1)S(1)}, u32[]{:S(2)}, u32[]{:S(2)}) collective-permute-start(bf16[2,1024]{1,0:T(2,128)(2,1)S(1)} %get-tuple-element.193), channel_id=1, source_target_pairs={{0,16},{16,32},{32,48},{48,64},{64,80},{80,96},{96,112},{112,128},... | collective-permute-start | bytes 12296 | tf_op jit(solution)/shard_map/while/body/eval_jaxpr/ppermute | solution.py:10
  411.8 4.2 collective-permute-start
  416.1 2.4 collective-permute-done
  418.6 2.5 collective-permute-start
  421.1 4.5 collective-permute-done
  425.7 1.9 collective-permute-start
  427.7 5.1 collective-permute-done
  432.9 1.9 collective-permute-start
  434.9 5.1 collective-permute-done
  440.1 1.9 collective-permute-start
  442.0 5.1 collective-permute-done
  447.2 1.9 collective-permute-start
  449.2 5.1 collective-permute-done
  454.4 1.9 collective-permute-start
  456.4 5.1 collective-permute-done
  461.6 1.9 collective-permute-start
  463.5 5.1 collective-permute-done
  468.8 1.9 collective-permute-start
  470.7 5.1 collective-permute-done
  477.9 5.1 collective-permute-done
  485.1 5.1 collective-permute-done
  492.2 5.1 collective-permute-done
  499.4 5.1 collective-permute-done
  506.6 5.1 collective-permute-done
  513.7 5.1 collective-permute-done
  520.9 5.1 collective-permute-done
  528.1 5.1 collective-permute-done
  533.3 1.9 collective-permute-start
  535.3 5.1 collective-permute-done
  542.4 5.1 collective-permute-done
  549.6 5.1 collective-permute-done
  556.8 5.1 collective-permute-done
  562.0 1.9 collective-permute-start
  563.9 5.1 collective-permute-done
  571.1 5.1 collective-permute-done
  578.3 5.1 collective-permute-done
  585.5 5.1 collective-permute-done
  592.6 5.1 collective-permute-done
  599.8 5.1 collective-permute-done
  607.0 5.1 collective-permute-done
  614.2 5.1 collective-permute-done
  621.3 5.1 collective-permute-done
  (109 shorter events, 50.9 us)
Async XLA Ops:
  7.2 1.1 copy-start
  7.2 175.1 %copy-start.1 = (bf16[1024,256]{1,0:T(8,128)(2,1)S(1)}, bf16[1024,256]{1,0:T(8,128)(2,1)}, u32[]{:S(2)}) copy-start(bf16[1024,256]{1,0:T(8,128)(2,1)} %param.8) | copy-start | bytes 1572868
  7.2 172.2 %all-reduce.4.cloned.1.call-start = ((), (), s32[]{:S(2)}) async-start(), calls=%async_computation | async-start | bytes 1048576 | tf_op jit(solution)/shard_map/psum | solution.py:53
  10.2 342.3 %all-reduce.6.cloned.1.call-start = ((), (), s32[]{:S(2)}) async-start(), calls=%async_computation.1 | async-start | bytes 262144
  390.6 236.7 %copy-start.2 = (bf16[2,1024]{1,0:T(2,128)(2,1)}, bf16[2,1024]{1,0:T(2,128)(2,1)S(1)}, u32[]{:S(2)}) copy-start(bf16[2,1024]{1,0:T(2,128)(2,1)S(1)} %multiply_convert_fusion) | copy-start | bytes 12292
  390.7 21.0 %collective-permute-start = (bf16[2,1024]{1,0:T(2,128)(2,1)S(1)}, bf16[2,1024]{1,0:T(2,128)(2,1)S(1)}, u32[]{:S(2)}, u32[]{:S(2)}) collective-permute-start(bf16[2,1024]{1,0:T(2,128)(2,1)S(1)} %get-tuple-element.193), channel_id=1, source_target_pairs={{0,16},{16,32},{32,48},{48,64},{64,80},{80,96},{96,112},{112,128},... | collective-permute-start | bytes 12296 | tf_op jit(solution)/shard_map/while/body/eval_jaxpr/ppermute | solution.py:10
  411.8 6.6 %collective-permute-start = (bf16[2,1024]{1,0:T(2,128)(2,1)S(1)}, bf16[2,1024]{1,0:T(2,128)(2,1)S(1)}, u32[]{:S(2)}, u32[]{:S(2)}) collective-permute-start(bf16[2,1024]{1,0:T(2,128)(2,1)S(1)} %get-tuple-element.193), channel_id=1, source_target_pairs={{0,16},{16,32},{32,48},{48,64},{64,80},{80,96},{96,112},{112,128},... | collective-permute-start | bytes 12296 | tf_op jit(solution)/shard_map/while/body/eval_jaxpr/ppermute | solution.py:10
  418.6 7.0 %collective-permute-start = (bf16[2,1024]{1,0:T(2,128)(2,1)S(1)}, bf16[2,1024]{1,0:T(2,128)(2,1)S(1)}, u32[]{:S(2)}, u32[]{:S(2)}) collective-permute-start(bf16[2,1024]{1,0:T(2,128)(2,1)S(1)} %get-tuple-element.193), channel_id=1, source_target_pairs={{0,16},{16,32},{32,48},{48,64},{64,80},{80,96},{96,112},{112,128},... | collective-permute-start | bytes 12296 | tf_op jit(solution)/shard_map/while/body/eval_jaxpr/ppermute | solution.py:10
  425.7 7.0 %collective-permute-start = (bf16[2,1024]{1,0:T(2,128)(2,1)S(1)}, bf16[2,1024]{1,0:T(2,128)(2,1)S(1)}, u32[]{:S(2)}, u32[]{:S(2)}) collective-permute-start(bf16[2,1024]{1,0:T(2,128)(2,1)S(1)} %get-tuple-element.193), channel_id=1, source_target_pairs={{0,16},{16,32},{32,48},{48,64},{64,80},{80,96},{96,112},{112,128},... | collective-permute-start | bytes 12296 | tf_op jit(solution)/shard_map/while/body/eval_jaxpr/ppermute | solution.py:10
  432.9 7.0 %collective-permute-start = (bf16[2,1024]{1,0:T(2,128)(2,1)S(1)}, bf16[2,1024]{1,0:T(2,128)(2,1)S(1)}, u32[]{:S(2)}, u32[]{:S(2)}) collective-permute-start(bf16[2,1024]{1,0:T(2,128)(2,1)S(1)} %get-tuple-element.193), channel_id=1, source_target_pairs={{0,16},{16,32},{32,48},{48,64},{64,80},{80,96},{96,112},{112,128},... | collective-permute-start | bytes 12296 | tf_op jit(solution)/shard_map/while/body/eval_jaxpr/ppermute | solution.py:10
  440.1 7.0 %collective-permute-start = (bf16[2,1024]{1,0:T(2,128)(2,1)S(1)}, bf16[2,1024]{1,0:T(2,128)(2,1)S(1)}, u32[]{:S(2)}, u32[]{:S(2)}) collective-permute-start(bf16[2,1024]{1,0:T(2,128)(2,1)S(1)} %get-tuple-element.193), channel_id=1, source_target_pairs={{0,16},{16,32},{32,48},{48,64},{64,80},{80,96},{96,112},{112,128},... | collective-permute-start | bytes 12296 | tf_op jit(solution)/shard_map/while/body/eval_jaxpr/ppermute | solution.py:10
  447.2 7.0 %collective-permute-start = (bf16[2,1024]{1,0:T(2,128)(2,1)S(1)}, bf16[2,1024]{1,0:T(2,128)(2,1)S(1)}, u32[]{:S(2)}, u32[]{:S(2)}) collective-permute-start(bf16[2,1024]{1,0:T(2,128)(2,1)S(1)} %get-tuple-element.193), channel_id=1, source_target_pairs={{0,16},{16,32},{32,48},{48,64},{64,80},{80,96},{96,112},{112,128},... | collective-permute-start | bytes 12296 | tf_op jit(solution)/shard_map/while/body/eval_jaxpr/ppermute | solution.py:10
  454.4 7.0 %collective-permute-start = (bf16[2,1024]{1,0:T(2,128)(2,1)S(1)}, bf16[2,1024]{1,0:T(2,128)(2,1)S(1)}, u32[]{:S(2)}, u32[]{:S(2)}) collective-permute-start(bf16[2,1024]{1,0:T(2,128)(2,1)S(1)} %get-tuple-element.193), channel_id=1, source_target_pairs={{0,16},{16,32},{32,48},{48,64},{64,80},{80,96},{96,112},{112,128},... | collective-permute-start | bytes 12296 | tf_op jit(solution)/shard_map/while/body/eval_jaxpr/ppermute | solution.py:10
  461.6 7.0 %collective-permute-start = (bf16[2,1024]{1,0:T(2,128)(2,1)S(1)}, bf16[2,1024]{1,0:T(2,128)(2,1)S(1)}, u32[]{:S(2)}, u32[]{:S(2)}) collective-permute-start(bf16[2,1024]{1,0:T(2,128)(2,1)S(1)} %get-tuple-element.193), channel_id=1, source_target_pairs={{0,16},{16,32},{32,48},{48,64},{64,80},{80,96},{96,112},{112,128},... | collective-permute-start | bytes 12296 | tf_op jit(solution)/shard_map/while/body/eval_jaxpr/ppermute | solution.py:10
  468.8 7.0 %collective-permute-start = (bf16[2,1024]{1,0:T(2,128)(2,1)S(1)}, bf16[2,1024]{1,0:T(2,128)(2,1)S(1)}, u32[]{:S(2)}, u32[]{:S(2)}) collective-permute-start(bf16[2,1024]{1,0:T(2,128)(2,1)S(1)} %get-tuple-element.193), channel_id=1, source_target_pairs={{0,16},{16,32},{32,48},{48,64},{64,80},{80,96},{96,112},{112,128},... | collective-permute-start | bytes 12296 | tf_op jit(solution)/shard_map/while/body/eval_jaxpr/ppermute | solution.py:10
  475.9 7.0 %collective-permute-start = (bf16[2,1024]{1,0:T(2,128)(2,1)S(1)}, bf16[2,1024]{1,0:T(2,128)(2,1)S(1)}, u32[]{:S(2)}, u32[]{:S(2)}) collective-permute-start(bf16[2,1024]{1,0:T(2,128)(2,1)S(1)} %get-tuple-element.193), channel_id=1, source_target_pairs={{0,16},{16,32},{32,48},{48,64},{64,80},{80,96},{96,112},{112,128},... | collective-permute-start | bytes 12296 | tf_op jit(solution)/shard_map/while/body/eval_jaxpr/ppermute | solution.py:10
  483.1 7.0 %collective-permute-start = (bf16[2,1024]{1,0:T(2,128)(2,1)S(1)}, bf16[2,1024]{1,0:T(2,128)(2,1)S(1)}, u32[]{:S(2)}, u32[]{:S(2)}) collective-permute-start(bf16[2,1024]{1,0:T(2,128)(2,1)S(1)} %get-tuple-element.193), channel_id=1, source_target_pairs={{0,16},{16,32},{32,48},{48,64},{64,80},{80,96},{96,112},{112,128},... | collective-permute-start | bytes 12296 | tf_op jit(solution)/shard_map/while/body/eval_jaxpr/ppermute | solution.py:10
  490.3 7.0 %collective-permute-start = (bf16[2,1024]{1,0:T(2,128)(2,1)S(1)}, bf16[2,1024]{1,0:T(2,128)(2,1)S(1)}, u32[]{:S(2)}, u32[]{:S(2)}) collective-permute-start(bf16[2,1024]{1,0:T(2,128)(2,1)S(1)} %get-tuple-element.193), channel_id=1, source_target_pairs={{0,16},{16,32},{32,48},{48,64},{64,80},{80,96},{96,112},{112,128},... | collective-permute-start | bytes 12296 | tf_op jit(solution)/shard_map/while/body/eval_jaxpr/ppermute | solution.py:10
  497.5 7.0 %collective-permute-start = (bf16[2,1024]{1,0:T(2,128)(2,1)S(1)}, bf16[2,1024]{1,0:T(2,128)(2,1)S(1)}, u32[]{:S(2)}, u32[]{:S(2)}) collective-permute-start(bf16[2,1024]{1,0:T(2,128)(2,1)S(1)} %get-tuple-element.193), channel_id=1, source_target_pairs={{0,16},{16,32},{32,48},{48,64},{64,80},{80,96},{96,112},{112,128},... | collective-permute-start | bytes 12296 | tf_op jit(solution)/shard_map/while/body/eval_jaxpr/ppermute | solution.py:10
  504.6 7.0 %collective-permute-start = (bf16[2,1024]{1,0:T(2,128)(2,1)S(1)}, bf16[2,1024]{1,0:T(2,128)(2,1)S(1)}, u32[]{:S(2)}, u32[]{:S(2)}) collective-permute-start(bf16[2,1024]{1,0:T(2,128)(2,1)S(1)} %get-tuple-element.193), channel_id=1, source_target_pairs={{0,16},{16,32},{32,48},{48,64},{64,80},{80,96},{96,112},{112,128},... | collective-permute-start | bytes 12296 | tf_op jit(solution)/shard_map/while/body/eval_jaxpr/ppermute | solution.py:10
  511.8 7.0 %collective-permute-start = (bf16[2,1024]{1,0:T(2,128)(2,1)S(1)}, bf16[2,1024]{1,0:T(2,128)(2,1)S(1)}, u32[]{:S(2)}, u32[]{:S(2)}) collective-permute-start(bf16[2,1024]{1,0:T(2,128)(2,1)S(1)} %get-tuple-element.193), channel_id=1, source_target_pairs={{0,16},{16,32},{32,48},{48,64},{64,80},{80,96},{96,112},{112,128},... | collective-permute-start | bytes 12296 | tf_op jit(solution)/shard_map/while/body/eval_jaxpr/ppermute | solution.py:10
  519.0 7.0 %collective-permute-start = (bf16[2,1024]{1,0:T(2,128)(2,1)S(1)}, bf16[2,1024]{1,0:T(2,128)(2,1)S(1)}, u32[]{:S(2)}, u32[]{:S(2)}) collective-permute-start(bf16[2,1024]{1,0:T(2,128)(2,1)S(1)} %get-tuple-element.193), channel_id=1, source_target_pairs={{0,16},{16,32},{32,48},{48,64},{64,80},{80,96},{96,112},{112,128},... | collective-permute-start | bytes 12296 | tf_op jit(solution)/shard_map/while/body/eval_jaxpr/ppermute | solution.py:10
  526.1 7.0 %collective-permute-start = (bf16[2,1024]{1,0:T(2,128)(2,1)S(1)}, bf16[2,1024]{1,0:T(2,128)(2,1)S(1)}, u32[]{:S(2)}, u32[]{:S(2)}) collective-permute-start(bf16[2,1024]{1,0:T(2,128)(2,1)S(1)} %get-tuple-element.193), channel_id=1, source_target_pairs={{0,16},{16,32},{32,48},{48,64},{64,80},{80,96},{96,112},{112,128},... | collective-permute-start | bytes 12296 | tf_op jit(solution)/shard_map/while/body/eval_jaxpr/ppermute | solution.py:10
  533.3 7.0 %collective-permute-start = (bf16[2,1024]{1,0:T(2,128)(2,1)S(1)}, bf16[2,1024]{1,0:T(2,128)(2,1)S(1)}, u32[]{:S(2)}, u32[]{:S(2)}) collective-permute-start(bf16[2,1024]{1,0:T(2,128)(2,1)S(1)} %get-tuple-element.193), channel_id=1, source_target_pairs={{0,16},{16,32},{32,48},{48,64},{64,80},{80,96},{96,112},{112,128},... | collective-permute-start | bytes 12296 | tf_op jit(solution)/shard_map/while/body/eval_jaxpr/ppermute | solution.py:10
  540.5 7.0 %collective-permute-start = (bf16[2,1024]{1,0:T(2,128)(2,1)S(1)}, bf16[2,1024]{1,0:T(2,128)(2,1)S(1)}, u32[]{:S(2)}, u32[]{:S(2)}) collective-permute-start(bf16[2,1024]{1,0:T(2,128)(2,1)S(1)} %get-tuple-element.193), channel_id=1, source_target_pairs={{0,16},{16,32},{32,48},{48,64},{64,80},{80,96},{96,112},{112,128},... | collective-permute-start | bytes 12296 | tf_op jit(solution)/shard_map/while/body/eval_jaxpr/ppermute | solution.py:10
  547.7 7.0 %collective-permute-start = (bf16[2,1024]{1,0:T(2,128)(2,1)S(1)}, bf16[2,1024]{1,0:T(2,128)(2,1)S(1)}, u32[]{:S(2)}, u32[]{:S(2)}) collective-permute-start(bf16[2,1024]{1,0:T(2,128)(2,1)S(1)} %get-tuple-element.193), channel_id=1, source_target_pairs={{0,16},{16,32},{32,48},{48,64},{64,80},{80,96},{96,112},{112,128},... | collective-permute-start | bytes 12296 | tf_op jit(solution)/shard_map/while/body/eval_jaxpr/ppermute | solution.py:10
  554.8 7.0 %collective-permute-start = (bf16[2,1024]{1,0:T(2,128)(2,1)S(1)}, bf16[2,1024]{1,0:T(2,128)(2,1)S(1)}, u32[]{:S(2)}, u32[]{:S(2)}) collective-permute-start(bf16[2,1024]{1,0:T(2,128)(2,1)S(1)} %get-tuple-element.193), channel_id=1, source_target_pairs={{0,16},{16,32},{32,48},{48,64},{64,80},{80,96},{96,112},{112,128},... | collective-permute-start | bytes 12296 | tf_op jit(solution)/shard_map/while/body/eval_jaxpr/ppermute | solution.py:10
  562.0 7.0 %collective-permute-start = (bf16[2,1024]{1,0:T(2,128)(2,1)S(1)}, bf16[2,1024]{1,0:T(2,128)(2,1)S(1)}, u32[]{:S(2)}, u32[]{:S(2)}) collective-permute-start(bf16[2,1024]{1,0:T(2,128)(2,1)S(1)} %get-tuple-element.193), channel_id=1, source_target_pairs={{0,16},{16,32},{32,48},{48,64},{64,80},{80,96},{96,112},{112,128},... | collective-permute-start | bytes 12296 | tf_op jit(solution)/shard_map/while/body/eval_jaxpr/ppermute | solution.py:10
  569.2 7.0 %collective-permute-start = (bf16[2,1024]{1,0:T(2,128)(2,1)S(1)}, bf16[2,1024]{1,0:T(2,128)(2,1)S(1)}, u32[]{:S(2)}, u32[]{:S(2)}) collective-permute-start(bf16[2,1024]{1,0:T(2,128)(2,1)S(1)} %get-tuple-element.193), channel_id=1, source_target_pairs={{0,16},{16,32},{32,48},{48,64},{64,80},{80,96},{96,112},{112,128},... | collective-permute-start | bytes 12296 | tf_op jit(solution)/shard_map/while/body/eval_jaxpr/ppermute | solution.py:10
  576.3 7.0 %collective-permute-start = (bf16[2,1024]{1,0:T(2,128)(2,1)S(1)}, bf16[2,1024]{1,0:T(2,128)(2,1)S(1)}, u32[]{:S(2)}, u32[]{:S(2)}) collective-permute-start(bf16[2,1024]{1,0:T(2,128)(2,1)S(1)} %get-tuple-element.193), channel_id=1, source_target_pairs={{0,16},{16,32},{32,48},{48,64},{64,80},{80,96},{96,112},{112,128},... | collective-permute-start | bytes 12296 | tf_op jit(solution)/shard_map/while/body/eval_jaxpr/ppermute | solution.py:10
  583.5 7.0 %collective-permute-start = (bf16[2,1024]{1,0:T(2,128)(2,1)S(1)}, bf16[2,1024]{1,0:T(2,128)(2,1)S(1)}, u32[]{:S(2)}, u32[]{:S(2)}) collective-permute-start(bf16[2,1024]{1,0:T(2,128)(2,1)S(1)} %get-tuple-element.193), channel_id=1, source_target_pairs={{0,16},{16,32},{32,48},{48,64},{64,80},{80,96},{96,112},{112,128},... | collective-permute-start | bytes 12296 | tf_op jit(solution)/shard_map/while/body/eval_jaxpr/ppermute | solution.py:10
  590.7 7.0 %collective-permute-start = (bf16[2,1024]{1,0:T(2,128)(2,1)S(1)}, bf16[2,1024]{1,0:T(2,128)(2,1)S(1)}, u32[]{:S(2)}, u32[]{:S(2)}) collective-permute-start(bf16[2,1024]{1,0:T(2,128)(2,1)S(1)} %get-tuple-element.193), channel_id=1, source_target_pairs={{0,16},{16,32},{32,48},{48,64},{64,80},{80,96},{96,112},{112,128},... | collective-permute-start | bytes 12296 | tf_op jit(solution)/shard_map/while/body/eval_jaxpr/ppermute | solution.py:10
  597.9 7.0 %collective-permute-start = (bf16[2,1024]{1,0:T(2,128)(2,1)S(1)}, bf16[2,1024]{1,0:T(2,128)(2,1)S(1)}, u32[]{:S(2)}, u32[]{:S(2)}) collective-permute-start(bf16[2,1024]{1,0:T(2,128)(2,1)S(1)} %get-tuple-element.193), channel_id=1, source_target_pairs={{0,16},{16,32},{32,48},{48,64},{64,80},{80,96},{96,112},{112,128},... | collective-permute-start | bytes 12296 | tf_op jit(solution)/shard_map/while/body/eval_jaxpr/ppermute | solution.py:10
  605.0 7.0 %collective-permute-start = (bf16[2,1024]{1,0:T(2,128)(2,1)S(1)}, bf16[2,1024]{1,0:T(2,128)(2,1)S(1)}, u32[]{:S(2)}, u32[]{:S(2)}) collective-permute-start(bf16[2,1024]{1,0:T(2,128)(2,1)S(1)} %get-tuple-element.193), channel_id=1, source_target_pairs={{0,16},{16,32},{32,48},{48,64},{64,80},{80,96},{96,112},{112,128},... | collective-permute-start | bytes 12296 | tf_op jit(solution)/shard_map/while/body/eval_jaxpr/ppermute | solution.py:10
  612.2 7.0 %collective-permute-start = (bf16[2,1024]{1,0:T(2,128)(2,1)S(1)}, bf16[2,1024]{1,0:T(2,128)(2,1)S(1)}, u32[]{:S(2)}, u32[]{:S(2)}) collective-permute-start(bf16[2,1024]{1,0:T(2,128)(2,1)S(1)} %get-tuple-element.193), channel_id=1, source_target_pairs={{0,16},{16,32},{32,48},{48,64},{64,80},{80,96},{96,112},{112,128},... | collective-permute-start | bytes 12296 | tf_op jit(solution)/shard_map/while/body/eval_jaxpr/ppermute | solution.py:10
  619.4 7.0 %collective-permute-start = (bf16[2,1024]{1,0:T(2,128)(2,1)S(1)}, bf16[2,1024]{1,0:T(2,128)(2,1)S(1)}, u32[]{:S(2)}, u32[]{:S(2)}) collective-permute-start(bf16[2,1024]{1,0:T(2,128)(2,1)S(1)} %get-tuple-element.193), channel_id=1, source_target_pairs={{0,16},{16,32},{32,48},{48,64},{64,80},{80,96},{96,112},{112,128},... | collective-permute-start | bytes 12296 | tf_op jit(solution)/shard_map/while/body/eval_jaxpr/ppermute | solution.py:10
Sparse Core Ops, SparseCore 0:
  10.9 168.4 all-reduce.3
  183.9 168.5 all-reduce.5
where the time goes:
time: 638 us; the launch traced here: 634 us
  waiting for transfers between devices  484 us (76%)
  starting transfers between devices  80.7 us (13%)
  blocking collectives  35.5 us (6%)
  between operations  14.8 us (2%)
  matrix products  10.6 us (2%)
    psum x1, waiting for transfers between devices, per_device(): rank_full = lax.psum(rank_portion, 'mp')  167 us
    unnamed x3, waiting for transfers between devices  167 us
    ppermute x31, waiting for transfers between devices, from_behind(): return lax.ppermute(value, axis, pairs)  150 us
    ppermute x31, starting transfers between devices, from_behind(): return lax.ppermute(value, axis, pairs)  80.6 us
    all_gather x1, blocking collectives, per_device(): rows_unit = lax.all_gather(own_block, 'mp', axis=0, tiled=True)  35.5 us
  transfers between devices with their start and end apart: 33, of which 33 were waited for; matrix products, arithmetic and copies ran while one was open for 1% of the time, Pallas kernels for 0%

commit v1 on v0

v1 whole, which is shorter than its diff:
```python
import functools

import jax
import jax.numpy as jnp
from jax import lax
from jax.experimental import pallas as pl
from jax.experimental.pallas import tpu as pltpu
from jax.sharding import PartitionSpec as P

MESH = pl.DeviceIdType.MESH
NT = (((1,), (1,)), ((), ()))
LANES = 128


def unpack_signs(words):
    shape = (words.shape[0], 16, words.shape[1])
    offsets = lax.broadcasted_iota(jnp.int32, shape, 1)
    bits = jnp.bitwise_and(jnp.right_shift(words[:, None, :], offsets), 1)
    signs = (2 * bits - 1).astype(jnp.float32).astype(jnp.bfloat16)
    return signs.reshape(shape[0] * 16, shape[2])


def kernel(
    n_dp, n_mp, seq,
    act_hbm, grad_hbm, up_hbm, rank_words_hbm, feat_words_hbm, lengths,
    sketch_out, cos_out,
    act, grad, up, rank_words, feat_words, in_sem,
    sign_rank, sign_feat, right,
    part, part_in, rank_sum, raw, raw_in, mine, group, others, group_f, others_f,
    part_send, part_recv, rank_send, rank_recv, raw_send, raw_recv,
    group_send, group_recv, other_send, other_recv,
):
    my_dp = lax.axis_index("dp")
    me = lax.axis_index("mp")
    rows = act.shape[0] // n_mp
    own = rows // seq
    blocks = sign_feat.shape[0] // LANES
    width = own * blocks

    loads = [
        pltpu.make_async_copy(src, dst, in_sem.at[at])
        for at, (src, dst) in enumerate(
            [
                (up_hbm, up),
                (grad_hbm, grad),
                (feat_words_hbm, feat_words),
                (act_hbm, act),
                (rank_words_hbm, rank_words),
            ]
        )
    ]
    for load in loads:
        load.start()

    barrier = pltpu.get_barrier_semaphore()

    @pl.loop(1, n_mp)
    def _(step):
        pl.semaphore_signal(
            barrier, inc=1, device_id=(my_dp, lax.rem(me + step, n_mp)), device_id_type=MESH
        )

    @pl.loop(1, n_dp)
    def _(step):
        pl.semaphore_signal(
            barrier, inc=1, device_id=(lax.rem(my_dp + step, n_dp), me), device_id_type=MESH
        )

    loads[0].wait()
    loads[1].wait()
    pl.semaphore_wait(barrier, n_mp + n_dp - 2)

    def send_part(to):
        return pltpu.make_async_remote_copy(
            src_ref=part.at[to], dst_ref=part_in.at[me],
            send_sem=part_send.at[to], recv_sem=part_recv.at[me],
            device_id=(my_dp, to), device_id_type=MESH,
        )

    def from_part(source):
        return pltpu.make_async_remote_copy(
            src_ref=part.at[source], dst_ref=part_in.at[source],
            send_sem=part_send.at[source], recv_sem=part_recv.at[source],
            device_id=(my_dp, source), device_id_type=MESH,
        )

    @pl.loop(1, n_mp + 1)
    def _(step):
        to = lax.rem(me + step, n_mp)
        tokens = grad[pl.ds(pl.multiple_of(to * rows, rows), rows), :]
        part[to] = jnp.dot(tokens, up[...], preferred_element_type=jnp.float32).astype(jnp.bfloat16)

        @pl.when(step < n_mp)
        def _():
            send_part(to).start()

    for load in loads[2:]:
        load.wait()
    sign_feat[...] = unpack_signs(feat_words[...])
    sign_rank[...] = unpack_signs(rank_words[...])

    @pl.loop(0, 4)
    def _(step):
        at = pl.ds(pl.multiple_of(step * (act.shape[0] // 4), act.shape[0] // 4), act.shape[0] // 4)
        right[at, :] = lax.dot_general(
            act[at, :], sign_feat[...], NT, preferred_element_type=jnp.float32
        )

    part_in[me] = part[me]

    @pl.loop(1, n_mp)
    def _(step):
        from_part(lax.rem(me + step, n_mp)).wait_recv()

    total = part_in[0].astype(jnp.float32)
    for source in range(1, n_mp):
        total = total + part_in[source].astype(jnp.float32)
    slot = lax.broadcasted_iota(jnp.int32, (seq, LANES), 0)
    for example in range(own):
        live = (slot < lengths[me * own + example]).astype(jnp.float32)
        rank_sum[me, example * seq:(example + 1) * seq, :] = (
            total[example * seq:(example + 1) * seq, :] * live
        ).astype(jnp.bfloat16)

    def send_rank(to):
        return pltpu.make_async_remote_copy(
            src_ref=rank_sum.at[me], dst_ref=rank_sum.at[me],
            send_sem=rank_send.at[to], recv_sem=rank_recv.at[me],
            device_id=(my_dp, to), device_id_type=MESH,
        )

    def from_rank(source):
        return pltpu.make_async_remote_copy(
            src_ref=rank_sum.at[source], dst_ref=rank_sum.at[source],
            send_sem=rank_send.at[source], recv_sem=rank_recv.at[source],
            device_id=(my_dp, source), device_id_type=MESH,
        )

    @pl.loop(1, n_mp)
    def _(step):
        send_rank(lax.rem(me + step, n_mp)).start()

    def send_raw(to):
        return pltpu.make_async_remote_copy(
            src_ref=raw.at[to], dst_ref=raw_in.at[me],
            send_sem=raw_send.at[to], recv_sem=raw_recv.at[me],
            device_id=(my_dp, to), device_id_type=MESH,
        )

    def from_raw(source):
        return pltpu.make_async_remote_copy(
            src_ref=raw.at[source], dst_ref=raw_in.at[source],
            send_sem=raw_send.at[source], recv_sem=raw_recv.at[source],
            device_id=(my_dp, source), device_id_type=MESH,
        )

    def raw_chunk(owner):
        left = lax.dot_general(
            rank_sum[owner], sign_rank[...], NT, preferred_element_type=jnp.float32
        )
        product = left * right[pl.ds(pl.multiple_of(owner * rows, rows), rows), :]
        sums = product.reshape(own, seq, product.shape[1]).sum(axis=1)
        return [
            sums[example:example + 1, block * LANES:(block + 1) * LANES]
            for example in range(own)
            for block in range(blocks)
        ]

    for at, line in enumerate(raw_chunk(me)):
        raw_in[me, at:at + 1, :] = line

    @pl.loop(1, n_mp)
    def _(step):
        owner = lax.rem(me + step, n_mp)
        from_rank(owner).wait_recv()
        for at, line in enumerate(raw_chunk(owner)):
            raw[owner, at:at + 1, :] = line
        send_raw(owner).start()

    @pl.loop(1, n_mp)
    def _(step):
        from_raw(lax.rem(me + step, n_mp)).wait_recv()

    raw_sum = raw_in[0]
    for source in range(1, n_mp):
        raw_sum = raw_sum + raw_in[source]
    for example in range(own):
        part_rows = raw_sum[example * blocks:(example + 1) * blocks, :]
        mean = jnp.sum(part_rows * part_rows, keepdims=True) / (blocks * LANES)
        mine[example * blocks:(example + 1) * blocks, :] = part_rows * lax.rsqrt(mean + 1e-06)
    group[me] = mine[...].astype(jnp.bfloat16)
    others[my_dp] = mine[...].astype(jnp.bfloat16)

    def send_group(to):
        return pltpu.make_async_remote_copy(
            src_ref=group.at[me], dst_ref=group.at[me],
            send_sem=group_send.at[to], recv_sem=group_recv.at[me],
            device_id=(my_dp, to), device_id_type=MESH,
        )

    def from_group(source):
        return pltpu.make_async_remote_copy(
            src_ref=group.at[source], dst_ref=group.at[source],
            send_sem=group_send.at[source], recv_sem=group_recv.at[source],
            device_id=(my_dp, source), device_id_type=MESH,
        )

    def send_other(to):
        return pltpu.make_async_remote_copy(
            src_ref=others.at[my_dp], dst_ref=others.at[my_dp],
            send_sem=other_send.at[to], recv_sem=other_recv.at[my_dp],
            device_id=(to, me), device_id_type=MESH,
        )

    def from_other(source):
        return pltpu.make_async_remote_copy(
            src_ref=others.at[source], dst_ref=others.at[source],
            send_sem=other_send.at[source], recv_sem=other_recv.at[source],
            device_id=(source, me), device_id_type=MESH,
        )

    @pl.loop(1, n_dp)
    def _(step):
        send_other(lax.rem(my_dp + step, n_dp)).start()

    @pl.loop(1, n_mp)
    def _(step):
        send_group(lax.rem(me + step, n_mp)).start()

    sketch_out[...] = jnp.concatenate(
        [mine[pl.ds(block, own, stride=blocks), :] for block in range(blocks)], axis=1
    ).astype(jnp.bfloat16)

    @pl.loop(1, n_mp)
    def _(step):
        to = lax.rem(me + step, n_mp)
        send_part(to).wait_send()
        send_rank(to).wait_send()
        send_raw(to).wait_send()

    @pl.loop(1, n_mp)
    def _(step):
        from_group(lax.rem(me + step, n_mp)).wait_recv()

    group_f[...] = group[...].astype(jnp.float32).reshape(n_mp * width, LANES)

    @pl.loop(1, n_dp)
    def _(step):
        from_other(lax.rem(my_dp + step, n_dp)).wait_recv()

    others_f[...] = others[...].astype(jnp.float32).reshape(n_dp * width, LANES)

    for example in range(own):
        cosines = jnp.zeros((n_mp * own, n_dp), jnp.float32)
        for block in range(blocks):
            here = group_f[pl.ds(block, n_mp * own, stride=blocks), :].astype(jnp.bfloat16)
            there = others_f[pl.ds(example * blocks + block, n_dp, stride=width), :]
            cosines = cosines + lax.dot_general(
                here, there.astype(jnp.bfloat16), NT, preferred_element_type=jnp.float32
            )
        cos_out[example] = cosines / (blocks * LANES)

    @pl.loop(1, n_mp)
    def _(step):
        send_group(lax.rem(me + step, n_mp)).wait_send()

    @pl.loop(1, n_dp)
    def _(step):
        send_other(lax.rem(my_dp + step, n_dp)).wait_send()


def solution(mesh):
    n_dp, n_mp = mesh.shape["dp"], mesh.shape["mp"]

    def per_device(activations, gradients, up_matrix, rank_words, feat_words, lengths):
        examples = lengths.shape[0]
        tokens, features = activations.shape
        seq = tokens // examples
        own = examples // n_mp
        rank = up_matrix.shape[1]
        sketch = 16 * rank_words.shape[0]
        width = own * sketch // LANES
        rows = own * seq
        bf16, f32, dma = jnp.bfloat16, jnp.float32, pltpu.SemaphoreType.DMA
        anywhere = pl.BlockSpec(memory_space=pl.ANY)
        sketches, cosines = pl.pallas_call(
            functools.partial(kernel, n_dp, n_mp, seq),
            out_shape=[
                jax.ShapeDtypeStruct((own, sketch), bf16),
                jax.ShapeDtypeStruct((own, examples, n_dp), f32),
            ],
            in_specs=[anywhere] * 5 + [pl.BlockSpec(memory_space=pltpu.SMEM)],
            out_specs=[pl.BlockSpec(memory_space=pltpu.VMEM)] * 2,
            scratch_shapes=[
                pltpu.VMEM((tokens, features), bf16),
                pltpu.VMEM((tokens, features), bf16),
                pltpu.VMEM((features, rank), bf16),
                pltpu.VMEM(rank_words.shape, jnp.int32),
                pltpu.VMEM(feat_words.shape, jnp.int32),
                dma((5,)),
                pltpu.VMEM((sketch, rank), bf16),
                pltpu.VMEM((sketch, features), bf16),
                pltpu.VMEM((tokens, sketch), f32),
                pltpu.VMEM((n_mp, rows, rank), bf16),
                pltpu.VMEM((n_mp, rows, rank), bf16),
                pltpu.VMEM((n_mp, rows, rank), bf16),
                pltpu.VMEM((n_mp, width, LANES), f32),
                pltpu.VMEM((n_mp, width, LANES), f32),
                pltpu.VMEM((width, LANES), f32),
                pltpu.VMEM((n_mp, width, LANES), bf16),
                pltpu.VMEM((n_dp, width, LANES), bf16),
                pltpu.VMEM((n_mp * width, LANES), f32),
                pltpu.VMEM((n_dp * width, LANES), f32),
            ]
            + [dma((n_mp,))] * 8
            + [dma((n_dp,))] * 2,
            compiler_params=pltpu.CompilerParams(
                collective_id=0, has_side_effects=True, vmem_limit_bytes=32 * 1024 * 1024
            ),
        )(activations, gradients, up_matrix, rank_words, feat_words, lengths)
        return sketches, cosines.transpose(1, 2, 0)

    return jax.shard_map(
        per_device,
        mesh=mesh,
        in_specs=(P("dp", "mp"), P("dp", "mp"), P("mp", None), P(), P(None, "mp"), P("dp")),
        out_specs=(P(("dp", "mp"), None), P("dp", None, "mp")),
        check_vma=False,
    )
```

time: 638 us -> 58.4 us (0.09)
  waiting for transfers between devices: 484 us -> 0 us
  starting transfers between devices: 80.7 us -> 0 us
  Pallas kernels: 0 us -> 50.5 us
  blocking collectives: 35.5 us -> 0 us
  between operations: 14.8 us -> 0.65 us
  matrix products: 10.6 us -> 0 us
    psum x1 -> x0, waiting for transfers between devices: 167 us -> none  [per_device(): rank_full = lax.psum(rank_portion, 'mp')]
    unnamed x3 -> x0, waiting for transfers between devices: 167 us -> none
    ppermute x31 -> x0, waiting for transfers between devices: 150 us -> none  [from_behind(): return lax.ppermute(value, axis, pairs)]
    ppermute x31 -> x0, starting transfers between devices: 80.6 us -> none  [from_behind(): return lax.ppermute(value, axis, pairs)]
    pallas_call x0 -> x1, Pallas kernels: none -> 50.5 us  [per_device(): pl.pallas_call(functools.partial(kernel, n_dp, n_mp, seq), out_shape=[jax...]
    all_gather x1 -> x0, blocking collectives: 35.5 us -> none  [per_device(): rows_unit = lax.all_gather(own_block, 'mp', axis=0, tiled=True)]
    dot_general x35 -> x0, matrix products: 10.6 us -> none  [the longest x32 4.25 us: cos_tile(): lax.dot_general(rows_unit, other_block, (((1,), (1,)), ((), ())), preferr...]
  transfers between devices with their start and end apart: 33 -> 0, of which waited for: 33 -> 0; matrix products, arithmetic and copies ran while one was open for 1% -> 0% of each run, Pallas kernels for 0% -> 0%
where the time goes in v1:
time: 58.4 us; the launch traced here: 57.5 us
  Pallas kernels  50.5 us (86%)
  local copies, waits for them, and re-layouts  6.4 us (11%)
  between operations  0.65 us (1%)
    pallas_call x1, Pallas kernels, per_device(): pl.pallas_call(functools.partial(kernel, n_dp, n_mp, seq), out_shape=[jax...  50.5 us
    unnamed x14, local copies, waits for them, and re-layouts  6.4 us

profile of v1, /device:TPU:1, one launch (start us, length us, event | category | flops | bytes accessed | tf_op | source)
XLA Modules:
  0.0 57.5 jit_solution(1534856706532567755)
XLA Ops:
  0.6 0.0 copy-start
  0.6 1.0 %copy-done = bf16[1024,256]{1,0:T(8,128)(2,1)S(1)} copy-done((bf16[1024,256]{1,0:T(8,128)(2,1)S(1)}, bf16[1024,256]{1,0:T(8,128)(2,1)}, u32[]{:S(2)}) %copy-start) | copy-done | bytes 524312
  1.7 0.0 copy-start.1
  1.7 1.0 %copy-done.1 = bf16[1024,256]{1,0:T(8,128)(2,1)S(1)} copy-done((bf16[1024,256]{1,0:T(8,128)(2,1)S(1)}, bf16[1024,256]{1,0:T(8,128)(2,1)}, u32[]{:S(2)}) %copy-start.1) | copy-done | bytes 524312
  2.7 0.0 copy-start.2
  2.7 0.8 %copy-done.2 = bf16[256,128]{1,0:T(8,128)(2,1)S(1)} copy-done((bf16[256,128]{1,0:T(8,128)(2,1)S(1)}, bf16[256,128]{1,0:T(8,128)(2,1)}, u32[]{:S(2)}) %copy-start.2) | copy-done | bytes 65560
  3.6 0.0 copy-start.3
  3.6 0.8 %copy-done.3 = s32[64,256]{1,0:T(8,128)S(1)} copy-done((s32[64,256]{1,0:T(8,128)S(1)}, s32[64,256]{1,0:T(8,128)}, u32[]{:S(2)}) %copy-start.3) | copy-done | bytes 65560
  4.4 0.0 copy-start.4
  4.4 0.8 %copy-done.4 = s32[64,128]{1,0:T(8,128)S(1)} copy-done((s32[64,128]{1,0:T(8,128)S(1)}, s32[64,128]{1,0:T(8,128)}, u32[]{:S(2)}) %copy-start.4) | copy-done | bytes 32792
  5.2 0.0 copy-start.5
  5.2 0.7 %copy-done.5 = s32[32]{0:T(128)S(1)} copy-done((s32[32]{0:T(128)S(1)}, s32[32]{0:T(128)}, u32[]{:S(2)}) %copy-start.5) | copy-done | bytes 152
  5.8 50.5 %shard_map.77 = (bf16[2,1024]{1,0:T(2,128)(2,1)S(1)}, f32[2,32,32]{2,1,0:T(8,128)S(1)}) custom-call(bf16[1024,256]{1,0:T(8,128)(2,1)S(1)} %copy-done, bf16[1024,256]{1,0:T(8,128)(2,1)S(1)} %copy-done.1, bf16[256,128]{1,0:T(8,128)(2,1)S(1)} %copy-done.2, s32[64,128]{1,0:T(8,128)S(1)} %copy-done.4, s32[64,256]{1,0:T(8,128)S(1)} %copy-done.3, s32[32]{0:T(128)S(1)} %copy-done.5), custom_call_target="tpu_custom_call" | custom-call | tf_op jit(solution)/shard_map/pallas_call | solution.py:286
  56.3 0.6 %copy.8 = f32[32,32,2]{1,2,0:T(2,128)} copy(f32[32,32,2]{1,0,2:T(8,128)S(1)} %bitcast.1) | data formatting | bytes 16384
  57.0 0.6 %copy.10 = bf16[2,1024]{1,0:T(2,128)(2,1)} copy(bf16[2,1024]{1,0:T(2,128)(2,1)S(1)} %get-tuple-element.10) | data formatting | bytes 8192
Async XLA Ops:
  0.6 1.0 %copy-start = (bf16[1024,256]{1,0:T(8,128)(2,1)S(1)}, bf16[1024,256]{1,0:T(8,128)(2,1)}, u32[]{:S(2)}) copy-start(bf16[1024,256]{1,0:T(8,128)(2,1)} %act_hbm.1) | copy-start | bytes 1572868
  1.7 1.0 %copy-start.1 = (bf16[1024,256]{1,0:T(8,128)(2,1)S(1)}, bf16[1024,256]{1,0:T(8,128)(2,1)}, u32[]{:S(2)}) copy-start(bf16[1024,256]{1,0:T(8,128)(2,1)} %grad_hbm.1) | copy-start | bytes 1572868
  2.7 0.8 %copy-start.2 = (bf16[256,128]{1,0:T(8,128)(2,1)S(1)}, bf16[256,128]{1,0:T(8,128)(2,1)}, u32[]{:S(2)}) copy-start(bf16[256,128]{1,0:T(8,128)(2,1)} %up_hbm.1) | copy-start | bytes 196612
  3.6 0.8 %copy-start.3 = (s32[64,256]{1,0:T(8,128)S(1)}, s32[64,256]{1,0:T(8,128)}, u32[]{:S(2)}) copy-start(s32[64,256]{1,0:T(8,128)} %feat_words_hbm.1) | copy-start | bytes 196612
  4.4 0.8 %copy-start.4 = (s32[64,128]{1,0:T(8,128)S(1)}, s32[64,128]{1,0:T(8,128)}, u32[]{:S(2)}) copy-start(s32[64,128]{1,0:T(8,128)} %rank_words_hbm.1) | copy-start | bytes 98308
  5.2 0.7 %copy-start.5 = (s32[32]{0:T(128)S(1)}, s32[32]{0:T(128)}, u32[]{:S(2)}) copy-start(s32[32]{0:T(128)} %lengths.1) | copy-start | bytes 388

commit v2 on v0

v2 whole, which is shorter than its diff:
```python
import functools

import jax
import jax.numpy as jnp
from jax import lax
from jax.experimental import pallas as pl
from jax.experimental.pallas import tpu as pltpu
from jax.sharding import PartitionSpec as P

MESH = pl.DeviceIdType.MESH
NT = (((1,), (1,)), ((), ()))
LANES = 128
NX, NZ = 4, 4
NY, NC = 8, 4


def far_first(step, count):
    return count // 2 + (1 - 2 * (step % 2)) * ((step + 1) // 2)


def unpack_signs(words):
    shape = (words.shape[0], 16, words.shape[1])
    offsets = lax.broadcasted_iota(jnp.int32, shape, 1)
    bits = jnp.bitwise_and(jnp.right_shift(words[:, None, :], offsets), 1)
    signs = (2 * bits - 1).astype(jnp.float32).astype(jnp.bfloat16)
    return signs.reshape(shape[0] * 16, shape[2])


def kernel(
    n_dp, n_mp, seq,
    act_hbm, grad_hbm, up_hbm, rank_words_hbm, feat_words_hbm, lengths_hbm,
    sketch_out, cos_out,
    grad, up, rank_words, lengths, up_sem, grad_sem, rank_words_sem, lengths_sem,
    act_in, words_in, part, part_in, zsum, sign_rank, sign_feat, right, rank_pair,
    raw, raw_in, mine, group, others, group_f, others_f,
    act_send, act_recv, words_send, words_recv, part_send, part_recv, zsum_send, zsum_recv,
    raw_send, raw_recv, group_send, group_recv, other_send, other_recv,
):
    my_dp = lax.axis_index("dp")
    me = lax.axis_index("mp")
    x, z = me // NZ, me % NZ
    quarter = part.shape[1]
    examples = quarter // seq
    own = examples // NZ
    rows = own * seq
    sketch = sign_feat.shape[0]
    blocks = sketch // LANES
    width = own * blocks
    steps_x = [far_first(step, NX) for step in range(NX - 1)]
    steps_z = [far_first(step, NZ) for step in range(NZ - 1)]

    def rows_of(ref, at):
        return ref.at[pl.ds(pl.multiple_of(at * quarter, quarter), quarter), :]

    def remote(src, dst, send_sem, recv_sem, to_dp, to_mp):
        return pltpu.make_async_remote_copy(
            src_ref=src, dst_ref=dst, send_sem=send_sem, recv_sem=recv_sem,
            device_id=(to_dp, to_mp), device_id_type=MESH,
        )

    load_up = pltpu.make_async_copy(up_hbm, up, up_sem)
    load_grad = pltpu.make_async_copy(grad_hbm, grad, grad_sem)
    load_words = pltpu.make_async_copy(feat_words_hbm, words_in.at[x], words_recv.at[x])
    load_act = pltpu.make_async_copy(rows_of(act_hbm, x), act_in.at[x], act_recv.at[x])
    load_rank_words = pltpu.make_async_copy(rank_words_hbm, rank_words, rank_words_sem)
    load_lengths = pltpu.make_async_copy(lengths_hbm, lengths, lengths_sem)
    for load in (load_up, load_grad, load_words, load_act, load_rank_words, load_lengths):
        load.start()

    barrier = pltpu.get_barrier_semaphore()

    def mp_peer(step):
        return (x + far_first(step % NX, NX)) % NX * NZ + (z + far_first(step // NX, NZ)) % NZ

    def dp_peer(step):
        return (my_dp // NC + far_first(step // NC, NY)) % NY * NC + (
            my_dp % NC + (NC - 1 - step % NC)
        ) % NC

    @pl.loop(0, n_dp - 1)
    def _(step):
        pl.semaphore_signal(barrier, inc=1, device_id=(dp_peer(step), me), device_id_type=MESH)

    @pl.loop(0, n_mp - 1)
    def _(step):
        pl.semaphore_signal(barrier, inc=1, device_id=(my_dp, mp_peer(step)), device_id_type=MESH)

    load_up.wait()
    load_grad.wait()
    for step in range(NX):
        to = (x + far_first(step, NX)) % NX
        tokens = grad[pl.ds(pl.multiple_of(to * quarter, quarter), quarter), :]
        part[to] = jnp.dot(tokens, up[...], preferred_element_type=jnp.float32).astype(jnp.bfloat16)
    pl.semaphore_wait(barrier, n_mp + n_dp - 2)

    def send_part(to):
        return remote(
            part.at[to], part_in.at[x], part_send.at[to], part_recv.at[x], my_dp, to * NZ + z
        )

    def send_words(to):
        return remote(
            feat_words_hbm, words_in.at[x], words_send.at[to], words_recv.at[x], my_dp, to * NZ + z
        )

    def send_act(to):
        return remote(
            rows_of(act_hbm, to), act_in.at[x], act_send.at[to], act_recv.at[x], my_dp, to * NZ + z
        )

    for step in steps_x:
        send_part((x + step) % NX).start()
    for step in steps_x:
        send_words((x + step) % NX).start()
    for step in steps_x:
        send_act((x + step) % NX).start()

    load_rank_words.wait()
    signs = unpack_signs(rank_words[...])
    sign_rank[...] = jnp.concatenate([signs, signs], axis=1)

    def arrived(ref, sems, source):
        return remote(ref.at[source], ref.at[source], sems.at[source], sems.at[source], my_dp, me)

    load_words.wait()
    sign_feat[...] = unpack_signs(words_in[x])
    load_act.wait()
    right[...] = lax.dot_general(
        act_in[x], sign_feat[...], NT, preferred_element_type=jnp.float32
    )

    for step in steps_x:
        arrived(part_in, part_recv, (x + step) % NX).wait_recv()
    total = part[x].astype(jnp.float32)
    for step in steps_x:
        total = total + part_in[(x + step) % NX].astype(jnp.float32)
    zsum[z] = total.astype(jnp.bfloat16)

    def send_zsum(to):
        return remote(
            zsum.at[z], zsum.at[z], zsum_send.at[to], zsum_recv.at[z], my_dp, x * NZ + to
        )

    for step in steps_z:
        send_zsum((z + step) % NZ).start()

    for step in (1, 3, 2):
        source = (x + step) % NX
        arrived(words_in, words_recv, source).wait_recv()
        sign_feat[...] = unpack_signs(words_in[source])
        arrived(act_in, act_recv, source).wait_recv()
        right[...] += lax.dot_general(
            act_in[source], sign_feat[...], NT, preferred_element_type=jnp.float32
        )

    load_lengths.wait()
    for step in steps_z:
        arrived(zsum, zsum_recv, (z + step) % NZ).wait_recv()
    slot = lax.broadcasted_iota(jnp.int32, (seq, LANES), 0)
    for example in range(examples):
        at = slice(example * seq, (example + 1) * seq)
        total = zsum[0, at, :].astype(jnp.float32)
        for source in range(1, NZ):
            total = total + zsum[source, at, :].astype(jnp.float32)
        total = total * (slot < lengths[x * examples + example]).astype(jnp.float32)
        high = total.astype(jnp.bfloat16)
        rank_pair[at, :LANES] = high
        rank_pair[at, LANES:] = (total - high.astype(jnp.float32)).astype(jnp.bfloat16)

    def send_raw(to):
        return remote(
            raw.at[to], raw_in.at[z], raw_send.at[to], raw_recv.at[z], my_dp, x * NZ + to
        )

    for step in steps_z + [0]:
        owner = (z + step) % NZ
        at = pl.ds(pl.multiple_of(owner * rows, rows), rows)
        left = lax.dot_general(
            rank_pair[at, :], sign_rank[...], NT, preferred_element_type=jnp.float32
        )
        sums = (left * right[at, :]).reshape(own, seq, sketch).sum(axis=1)
        for example in range(own):
            for block in range(blocks):
                line = example * blocks + block
                raw[owner, line:line + 1, :] = sums[
                    example:example + 1, block * LANES:(block + 1) * LANES
                ]
        if step:
            send_raw(owner).start()

    raw_sum = raw[z]
    for step in steps_z:
        source = (z + step) % NZ
        arrived(raw_in, raw_recv, source).wait_recv()
        raw_sum = raw_sum + raw_in[source]
    for example in range(own):
        lines = raw_sum[example * blocks:(example + 1) * blocks, :]
        mean = jnp.sum(lines * lines, keepdims=True) / sketch
        mine[example * blocks:(example + 1) * blocks, :] = lines * lax.rsqrt(mean + 1e-06)
    group[me] = mine[...].astype(jnp.bfloat16)
    others[my_dp] = mine[...].astype(jnp.bfloat16)

    def send_group(to):
        return remote(
            group.at[me], group.at[me], group_send.at[to], group_recv.at[me], my_dp, to
        )

    def send_other(to):
        return remote(
            others.at[my_dp], others.at[my_dp], other_send.at[to], other_recv.at[my_dp], to, me
        )

    @pl.loop(0, n_dp - 1)
    def _(step):
        send_other(dp_peer(step)).start()

        @pl.when(step < n_mp - 1)
        def _():
            send_group(mp_peer(step)).start()

    sketch_out[...] = jnp.concatenate(
        [mine[pl.ds(block, own, stride=blocks), :] for block in range(blocks)], axis=1
    ).astype(jnp.bfloat16)

    for step in steps_x:
        to = (x + step) % NX
        send_part(to).wait_send()
        send_words(to).wait_send()
        send_act(to).wait_send()
    for step in steps_z:
        to = (z + step) % NZ
        send_zsum(to).wait_send()
        send_raw(to).wait_send()

    @pl.loop(0, n_mp - 1)
    def _(step):
        arrived(group, group_recv, mp_peer(step)).wait_recv()

    group_f[...] = group[...].astype(jnp.float32).reshape(n_mp * width, LANES)

    @pl.loop(0, n_dp - 1)
    def _(step):
        arrived(others, other_recv, dp_peer(step)).wait_recv()

    others_f[...] = others[...].astype(jnp.float32).reshape(n_dp * width, LANES)

    for example in range(own):
        cosines = jnp.zeros((n_mp * own, n_dp), jnp.float32)
        for block in range(blocks):
            here = group_f[pl.ds(block, n_mp * own, stride=blocks), :].astype(jnp.bfloat16)
            there = others_f[pl.ds(example * blocks + block, n_dp, stride=width), :]
            cosines = cosines + lax.dot_general(
                here, there.astype(jnp.bfloat16), NT, preferred_element_type=jnp.float32
            )
        cos_out[example] = cosines / sketch

    @pl.loop(0, n_mp - 1)
    def _(step):
        send_group(mp_peer(step)).wait_send()

    @pl.loop(0, n_dp - 1)
    def _(step):
        send_other(dp_peer(step)).wait_send()


def solution(mesh):
    n_dp, n_mp = mesh.shape["dp"], mesh.shape["mp"]

    def per_device(activations, gradients, up_matrix, rank_words, feat_words, lengths):
        examples = lengths.shape[0]
        tokens, features = activations.shape
        seq = tokens // examples
        own = examples // n_mp
        rank = up_matrix.shape[1]
        sketch = 16 * rank_words.shape[0]
        width = own * sketch // LANES
        quarter = tokens // NX
        bf16, f32, dma = jnp.bfloat16, jnp.float32, pltpu.SemaphoreType.DMA
        in_hbm = pl.BlockSpec(memory_space=pltpu.HBM)
        sketches, cosines = pl.pallas_call(
            functools.partial(kernel, n_dp, n_mp, seq),
            out_shape=[
                jax.ShapeDtypeStruct((own, sketch), bf16),
                jax.ShapeDtypeStruct((own, examples, n_dp), f32),
            ],
            in_specs=[in_hbm] * 6,
            out_specs=[pl.BlockSpec(memory_space=pltpu.VMEM)] * 2,
            scratch_shapes=[
                pltpu.VMEM((tokens, features), bf16),
                pltpu.VMEM((features, rank), bf16),
                pltpu.VMEM(rank_words.shape, jnp.int32),
                pltpu.SMEM((examples,), jnp.int32),
                dma(()),
                dma(()),
                dma(()),
                dma(()),
                pltpu.VMEM((NX, quarter, features), bf16),
                pltpu.VMEM((NX,) + feat_words.shape, jnp.int32),
                pltpu.VMEM((NX, quarter, rank), bf16),
                pltpu.VMEM((NX, quarter, rank), bf16),
                pltpu.VMEM((NZ, quarter, rank), bf16),
                pltpu.VMEM((sketch, 2 * rank), bf16),
                pltpu.VMEM((sketch, features), bf16),
                pltpu.VMEM((quarter, sketch), f32),
                pltpu.VMEM((quarter, 2 * rank), bf16),
                pltpu.VMEM((NZ, width, LANES), f32),
                pltpu.VMEM((NZ, width, LANES), f32),
                pltpu.VMEM((width, LANES), f32),
                pltpu.VMEM((n_mp, width, LANES), bf16),
                pltpu.VMEM((n_dp, width, LANES), bf16),
                pltpu.VMEM((n_mp * width, LANES), f32),
                pltpu.VMEM((n_dp * width, LANES), f32),
            ]
            + [dma((NX,))] * 6
            + [dma((NZ,))] * 4
            + [dma((n_mp,))] * 2
            + [dma((n_dp,))] * 2,
            compiler_params=pltpu.CompilerParams(
                collective_id=0, has_side_effects=True, vmem_limit_bytes=64 * 1024 * 1024
            ),
        )(activations, gradients, up_matrix, rank_words, feat_words, lengths)
        return sketches, cosines.transpose(1, 2, 0)

    return jax.shard_map(
        per_device,
        mesh=mesh,
        in_specs=(P("dp", "mp"), P("dp", "mp"), P("mp", None), P(), P(None, "mp"), P("dp")),
        out_specs=(P(("dp", "mp"), None), P("dp", None, "mp")),
        check_vma=False,
    )
```

time: 638 us -> 48.6 us (0.08)
  waiting for transfers between devices: 484 us -> 0 us
  starting transfers between devices: 80.7 us -> 0 us
  Pallas kernels: 0 us -> 45.8 us
  blocking collectives: 35.5 us -> 0 us
  between operations: 14.8 us -> 0.65 us
  matrix products: 10.6 us -> 0 us
    psum x1 -> x0, waiting for transfers between devices: 167 us -> none  [per_device(): rank_full = lax.psum(rank_portion, 'mp')]
    unnamed x3 -> x0, waiting for transfers between devices: 167 us -> none
    ppermute x31 -> x0, waiting for transfers between devices: 150 us -> none  [from_behind(): return lax.ppermute(value, axis, pairs)]
    ppermute x31 -> x0, starting transfers between devices: 80.6 us -> none  [from_behind(): return lax.ppermute(value, axis, pairs)]
    pallas_call x0 -> x1, Pallas kernels: none -> 45.8 us  [per_device(): pl.pallas_call(functools.partial(kernel, n_dp, n_mp, seq), out_shape=[jax...]
    all_gather x1 -> x0, blocking collectives: 35.5 us -> none  [per_device(): rows_unit = lax.all_gather(own_block, 'mp', axis=0, tiled=True)]
    dot_general x35 -> x0, matrix products: 10.6 us -> none  [the longest x32 4.25 us: cos_tile(): lax.dot_general(rows_unit, other_block, (((1,), (1,)), ((), ())), preferr...]
  transfers between devices with their start and end apart: 33 -> 0, of which waited for: 33 -> 0; matrix products, arithmetic and copies ran while one was open for 1% -> 0% of each run, Pallas kernels for 0% -> 0%
where the time goes in v2:
time: 48.6 us; the launch traced here: 48.5 us
  Pallas kernels  45.8 us (94%)
  local copies, waits for them, and re-layouts  2 us (4%)
  between operations  0.65 us (1%)
    pallas_call x1, Pallas kernels, per_device(): pl.pallas_call(functools.partial(kernel, n_dp, n_mp, seq), out_shape=[jax...  45.8 us
    unnamed x4, local copies, waits for them, and re-layouts  2 us

profile of v2, /device:TPU:1, one launch (start us, length us, event | category | flops | bytes accessed | tf_op | source)
XLA Modules:
  0.0 48.5 jit_solution(11912814967953843602)
XLA Ops:
  0.6 45.8 %shard_map.77 = (bf16[2,1024]{1,0:T(2,128)(2,1)}, f32[2,32,32]{2,1,0:T(8,128)}) custom-call(bf16[1024,256]{1,0:T(8,128)(2,1)} %act_hbm.1, bf16[1024,256]{1,0:T(8,128)(2,1)} %grad_hbm.1, bf16[256,128]{1,0:T(8,128)(2,1)} %up_hbm.1, s32[64,128]{1,0:T(8,128)} %rank_words_hbm.1, s32[64,256]{1,0:T(8,128)} %feat_words_hbm.1, s32[32]{0:T(128)} %lengths_hbm.1), custom_call_target="tpu_custom_call" | custom-call | tf_op jit(solution)/shard_map/pallas_call | solution.py:280
  46.5 0.0 copy-start
  46.5 1.4 %copy.8 = f32[32,32,2]{1,2,0:T(2,128)} copy(f32[32,32,2]{1,0,2:T(8,128)} %bitcast.1) | data formatting | bytes 16384
  47.9 0.0 copy-done
  47.9 0.6 %copy.10 = bf16[2,1024]{1,0:T(2,128)(2,1)} copy(bf16[2,1024]{1,0:T(2,128)(2,1)S(1)} %copy-done) | data formatting | bytes 8192
Async XLA Ops:
  46.5 1.4 %copy-start = (bf16[2,1024]{1,0:T(2,128)(2,1)S(1)}, bf16[2,1024]{1,0:T(2,128)(2,1)}, u32[]{:S(2)}) copy-start(bf16[2,1024]{1,0:T(2,128)(2,1)} %get-tuple-element.10) | copy-start | bytes 12292

commit v3 on v2

v3 whole, which is shorter than its diff:
```python
import functools

import jax
import jax.numpy as jnp
from jax import lax
from jax.experimental import pallas as pl
from jax.experimental.pallas import tpu as pltpu
from jax.sharding import PartitionSpec as P

MESH = pl.DeviceIdType.MESH
NT = (((1,), (1,)), ((), ()))
LANES = 128
NX, NZ = 4, 4
NY, NC = 8, 4


def far_first(count):
    return sorted(range(1, count), key=lambda step: -min(step, count - step))


def unpack_signs(words):
    words = words.astype(jnp.int32)
    shape = (words.shape[0], 16, words.shape[1])
    offsets = lax.broadcasted_iota(jnp.int32, shape, 1)
    bits = jnp.bitwise_and(jnp.right_shift(words[:, None, :], offsets), 1)
    signs = (2 * bits - 1).astype(jnp.float32).astype(jnp.bfloat16)
    return signs.reshape(shape[0] * 16, shape[2])


def kernel(
    n_dp, n_mp, seq,
    act_hbm, grad_hbm, up_hbm, rank_words_hbm, feat_words_hbm, lengths_hbm,
    sketch_out, cos_out,
    grad, up, rank_words, feat_words, lengths,
    up_sem, grad_sem, rank_words_sem, feat_words_sem, lengths_sem,
    act_in, words_in, part, part_in, zsum, sign_rank, sign_feat, right,
    raw, raw_in, mine, group, others, group_f, others_f,
    act_send, act_recv, words_send, words_recv, part_send, part_recv, zsum_send, zsum_recv,
    raw_send, raw_recv, group_send, group_recv, other_send, other_recv,
):
    my_dp = lax.axis_index("dp")
    me = lax.axis_index("mp")
    x, z = me // NZ, me % NZ
    y, core = my_dp // NC, my_dp % NC
    rows = part.shape[2]
    quarter = NZ * rows
    own = rows // seq
    examples = NZ * own
    sketch = sign_feat.shape[0]
    blocks = sketch // LANES
    width = own * blocks
    ring_x = [(x + step) % NX for step in far_first(NX)]
    ring_z = [(z + step) % NZ for step in far_first(NZ)]
    ring_y = [(y + step) % NY for step in far_first(NY)]
    ring_c = [(core + step) % NC for step in range(1, NC)]
    mp_peers = [to_x * NZ + to_z for to_z in ring_z for to_x in ring_x + [x]]
    mp_peers += [to_x * NZ + z for to_x in ring_x]
    dp_peers = [to_y * NC + to_c for to_y in ring_y for to_c in ring_c + [core]]
    dp_peers += [y * NC + to_c for to_c in ring_c]

    def rows_of(ref, at):
        return ref.at[pl.ds(pl.multiple_of(at * quarter, quarter), quarter), :]

    def remote(src, dst, send_sem, recv_sem, to_dp, to_mp):
        return pltpu.make_async_remote_copy(
            src_ref=src, dst_ref=dst, send_sem=send_sem, recv_sem=recv_sem,
            device_id=(to_dp, to_mp), device_id_type=MESH,
        )

    def arrived(ref, sem):
        return remote(ref, ref, sem, sem, my_dp, me)

    load_up = pltpu.make_async_copy(up_hbm, up, up_sem)
    load_grad = pltpu.make_async_copy(grad_hbm, grad, grad_sem)
    load_words = pltpu.make_async_copy(feat_words_hbm, feat_words, feat_words_sem)
    load_act = pltpu.make_async_copy(rows_of(act_hbm, x), act_in.at[x], act_recv.at[x])
    load_rank_words = pltpu.make_async_copy(rank_words_hbm, rank_words, rank_words_sem)
    load_lengths = pltpu.make_async_copy(lengths_hbm, lengths, lengths_sem)
    for load in (load_up, load_grad, load_words, load_act, load_rank_words, load_lengths):
        load.start()

    barrier = pltpu.get_barrier_semaphore()
    for to in mp_peers:
        pl.semaphore_signal(barrier, inc=1, device_id=(my_dp, to), device_id_type=MESH)
    for to in dp_peers:
        pl.semaphore_signal(barrier, inc=1, device_id=(to, me), device_id_type=MESH)

    load_up.wait()
    load_grad.wait()
    for to in ring_x + [x]:
        tokens = grad[pl.ds(pl.multiple_of(to * quarter, quarter), quarter), :]
        part[to] = (
            jnp.dot(tokens, up[...], preferred_element_type=jnp.float32)
            .astype(jnp.bfloat16)
            .reshape(NZ, rows, LANES)
        )
    load_words.wait()
    words_in[x] = feat_words[...].astype(jnp.int16)
    pl.semaphore_wait(barrier, n_mp + n_dp - 2)

    def send_part(to, piece):
        return remote(
            part.at[to, piece], part_in.at[x, piece],
            part_send.at[to, piece], part_recv.at[x, piece], my_dp, to * NZ + z,
        )

    def send_words(to):
        return remote(
            words_in.at[x], words_in.at[x], words_send.at[to], words_recv.at[x], my_dp, to * NZ + z
        )

    def send_act(to):
        return remote(
            rows_of(act_hbm, to), act_in.at[x], act_send.at[to], act_recv.at[x], my_dp, to * NZ + z
        )

    for piece in range(NZ):
        for to in ring_x:
            send_part(to, piece).start()
    for to in ring_x:
        send_words(to).start()
    for to in ring_x:
        send_act(to).start()

    load_rank_words.wait()
    signs = unpack_signs(rank_words[...])
    sign_rank[...] = jnp.concatenate([signs, signs], axis=1)
    sign_feat[...] = unpack_signs(words_in[x])
    load_act.wait()
    right[...] = lax.dot_general(
        act_in[x], sign_feat[...], NT, preferred_element_type=jnp.float32
    )

    def send_zsum(to, piece):
        return remote(
            zsum.at[z, piece], zsum.at[z, piece],
            zsum_send.at[to, piece], zsum_recv.at[z, piece], my_dp, x * NZ + to,
        )

    for piece in range(NZ):
        total = part[x, piece].astype(jnp.float32)
        for source in ring_x:
            arrived(part_in.at[source, piece], part_recv.at[source, piece]).wait_recv()
            total = total + part_in[source, piece].astype(jnp.float32)
        zsum[z, piece] = total.astype(jnp.bfloat16)
        for to in ring_z:
            send_zsum(to, piece).start()

    for source in ring_x[1:] + ring_x[:1]:
        arrived(words_in.at[source], words_recv.at[source]).wait_recv()
        sign_feat[...] = unpack_signs(words_in[source])
        arrived(act_in.at[source], act_recv.at[source]).wait_recv()
        right[...] += lax.dot_general(
            act_in[source], sign_feat[...], NT, preferred_element_type=jnp.float32
        )

    load_lengths.wait()
    slot = lax.broadcasted_iota(jnp.int32, (seq, LANES), 0)

    def send_raw(to):
        return remote(
            raw.at[to], raw_in.at[z], raw_send.at[to], raw_recv.at[z], my_dp, x * NZ + to
        )

    for piece in range(NZ):
        total = zsum[z, piece].astype(jnp.float32)
        for source in ring_z:
            arrived(zsum.at[source, piece], zsum_recv.at[source, piece]).wait_recv()
            total = total + zsum[source, piece].astype(jnp.float32)
        live = jnp.concatenate(
            [
                (slot < lengths[x * examples + piece * own + example]).astype(jnp.float32)
                for example in range(own)
            ]
        )
        total = total * live
        high = total.astype(jnp.bfloat16)
        low = (total - high.astype(jnp.float32)).astype(jnp.bfloat16)
        left = lax.dot_general(
            jnp.concatenate([high, low], axis=1), sign_rank[...], NT,
            preferred_element_type=jnp.float32,
        )
        product = left * right[piece * rows:(piece + 1) * rows, :]
        sums = product.reshape(own, seq, sketch).sum(axis=1)
        for example in range(own):
            for block in range(blocks):
                line = example * blocks + block
                raw[piece, line:line + 1, :] = sums[
                    example:example + 1, block * LANES:(block + 1) * LANES
                ]

        @pl.when(z != piece)
        def _():
            send_raw(piece).start()

    raw_sum = raw[z]
    for source in ring_z:
        arrived(raw_in.at[source], raw_recv.at[source]).wait_recv()
        raw_sum = raw_sum + raw_in[source]
    for example in range(own):
        lines = raw_sum[example * blocks:(example + 1) * blocks, :]
        mean = jnp.sum(lines * lines, keepdims=True) / sketch
        mine[example * blocks:(example + 1) * blocks, :] = lines * lax.rsqrt(mean + 1e-06)
    group[me] = mine[...].astype(jnp.bfloat16)
    others[my_dp] = mine[...].astype(jnp.bfloat16)

    for at, to in enumerate(dp_peers):
        remote(
            others.at[my_dp], others.at[my_dp], other_send, other_recv, to, me
        ).start()
        if at < len(mp_peers):
            remote(
                group.at[me], group.at[me], group_send, group_recv, my_dp, mp_peers[at]
            ).start()

    sketch_out[...] = jnp.concatenate(
        [mine[pl.ds(block, own, stride=blocks), :] for block in range(blocks)], axis=1
    ).astype(jnp.bfloat16)

    for to in ring_x:
        for piece in range(NZ):
            send_part(to, piece).wait_send()
        send_words(to).wait_send()
        send_act(to).wait_send()
    for to in ring_z:
        for piece in range(NZ):
            send_zsum(to, piece).wait_send()
        send_raw(to).wait_send()
    remote(
        group.at[pl.ds(0, n_mp - 1)], group.at[pl.ds(0, n_mp - 1)], group_send, group_recv, my_dp, me
    ).wait()
    group_f[...] = group[...].astype(jnp.float32).reshape(n_mp * width, LANES)
    remote(
        others.at[pl.ds(0, n_dp - 1)], others.at[pl.ds(0, n_dp - 1)], other_send, other_recv, my_dp, me
    ).wait()
    others_f[...] = others[...].astype(jnp.float32).reshape(n_dp * width, LANES)

    for example in range(own):
        cosines = jnp.zeros((n_mp * own, n_dp), jnp.float32)
        for block in range(blocks):
            here = group_f[pl.ds(block, n_mp * own, stride=blocks), :].astype(jnp.bfloat16)
            there = others_f[pl.ds(example * blocks + block, n_dp, stride=width), :]
            cosines = cosines + lax.dot_general(
                here, there.astype(jnp.bfloat16), NT, preferred_element_type=jnp.float32
            )
        cos_out[:, example, :] = cosines / sketch


def solution(mesh):
    n_dp, n_mp = mesh.shape["dp"], mesh.shape["mp"]

    def per_device(activations, gradients, up_matrix, rank_words, feat_words, lengths):
        examples = lengths.shape[0]
        tokens, features = activations.shape
        seq = tokens // examples
        own = examples // n_mp
        rank = up_matrix.shape[1]
        sketch = 16 * rank_words.shape[0]
        width = own * sketch // LANES
        quarter = tokens // NX
        pieces = (NX, NZ, own * seq, rank)
        bf16, f32, dma = jnp.bfloat16, jnp.float32, pltpu.SemaphoreType.DMA
        in_hbm = pl.BlockSpec(memory_space=pltpu.HBM)
        sketches, cosines = pl.pallas_call(
            functools.partial(kernel, n_dp, n_mp, seq),
            out_shape=[
                pltpu.VMEM((own, sketch), bf16),
                pltpu.VMEM((examples, own, n_dp), f32),
            ],
            in_specs=[in_hbm] * 6,
            out_specs=[pl.BlockSpec(memory_space=pltpu.VMEM)] * 2,
            scratch_shapes=[
                pltpu.VMEM((tokens, features), bf16),
                pltpu.VMEM((features, rank), bf16),
                pltpu.VMEM(rank_words.shape, jnp.int32),
                pltpu.VMEM(feat_words.shape, jnp.int32),
                pltpu.SMEM((examples,), jnp.int32),
                dma(()),
                dma(()),
                dma(()),
                dma(()),
                dma(()),
                pltpu.VMEM((NX, quarter, features), bf16),
                pltpu.VMEM((NX,) + feat_words.shape, jnp.int16),
                pltpu.VMEM(pieces, bf16),
                pltpu.VMEM(pieces, bf16),
                pltpu.VMEM((NZ,) + pieces[1:], bf16),
                pltpu.VMEM((sketch, 2 * rank), bf16),
                pltpu.VMEM((sketch, features), bf16),
                pltpu.VMEM((quarter, sketch), f32),
                pltpu.VMEM((NZ, width, LANES), f32),
                pltpu.VMEM((NZ, width, LANES), f32),
                pltpu.VMEM((width, LANES), f32),
                pltpu.VMEM((n_mp, width, LANES), bf16),
                pltpu.VMEM((n_dp, width, LANES), bf16),
                pltpu.VMEM((n_mp * width, LANES), f32),
                pltpu.VMEM((n_dp * width, LANES), f32),
            ]
            + [dma((NX,))] * 4
            + [dma((NX, NZ))] * 2
            + [dma((NZ, NZ))] * 2
            + [dma((NZ,))] * 2
            + [dma(())] * 4,
            compiler_params=pltpu.CompilerParams(
                collective_id=0, has_side_effects=True, vmem_limit_bytes=48 * 1024 * 1024
            ),
        )(*[pltpu.with_memory_space_constraint(each, pltpu.HBM) for each in (activations, gradients, up_matrix, rank_words, feat_words, lengths)])
        return sketches, cosines.transpose(0, 2, 1)

    return jax.shard_map(
        per_device,
        mesh=mesh,
        in_specs=(P("dp", "mp"), P("dp", "mp"), P("mp", None), P(), P(None, "mp"), P("dp")),
        out_specs=(P(("dp", "mp"), None), P("dp", None, "mp")),
        check_vma=False,
    )
```

time: 48.6 us -> 41.7 us (0.86)
  Pallas kernels: 45.8 us -> 39.7 us
  local copies, waits for them, and re-layouts: 2 us -> 1.21 us
    pallas_call x1, Pallas kernels: 45.8 us -> 39.7 us  [per_device(): pl.pallas_call(functools.partial(kernel, n_dp, n_mp, seq), out_shape=[plt...]
    unnamed x4 -> x2, local copies, waits for them, and re-layouts: 2 us -> 1.21 us
where the time goes in v3:
time: 41.7 us; the launch traced here: 41.5 us
  Pallas kernels  39.7 us (95%)
  local copies, waits for them, and re-layouts  1.21 us (3%)
  between operations  0.64 us (2%)
    pallas_call x1, Pallas kernels, per_device(): pl.pallas_call(functools.partial(kernel, n_dp, n_mp, seq), out_shape=[plt...  39.7 us
    unnamed x2, local copies, waits for them, and re-layouts  1.21 us

profile of v3, /device:TPU:1, one launch (start us, length us, event | category | flops | bytes accessed | tf_op | source)
XLA Modules:
  0.0 41.5 jit_solution(7576029821553455838)
XLA Ops:
  0.6 39.7 %shard_map.77 = (bf16[2,1024]{1,0:T(2,128)(2,1)S(1)}, f32[32,2,32]{2,1,0:T(2,128)S(1)}) custom-call(bf16[1024,256]{1,0:T(8,128)(2,1)} %act_hbm.1, bf16[1024,256]{1,0:T(8,128)(2,1)} %grad_hbm.1, bf16[256,128]{1,0:T(8,128)(2,1)} %up_hbm.1, s32[64,128]{1,0:T(8,128)} %rank_words_hbm.1, s32[64,256]{1,0:T(8,128)} %feat_words_hbm.1, s32[32]{0:T(128)} %lengths_hbm.1), custom_call_target="tpu_custom_call" | custom-call | tf_op jit(solution)/shard_map/pallas_call | solution.py:264
  40.3 0.6 %copy.10 = bf16[2,1024]{1,0:T(2,128)(2,1)} copy(bf16[2,1024]{1,0:T(2,128)(2,1)S(1)} %get-tuple-element.6) | data formatting | bytes 8192
  40.9 0.6 %copy.11 = f32[32,32,2]{1,2,0:T(2,128)} copy(f32[32,32,2]{1,2,0:T(2,128)S(1)} %bitcast.1) | data formatting | bytes 16384

commit v4 on v3

--- a/solution.py
+++ b/solution.py
@@ -33,10 +33,12 @@
     sketch_out, cos_out,
     grad, up, rank_words, feat_words, lengths,
     up_sem, grad_sem, rank_words_sem, feat_words_sem, lengths_sem,
-    act_in, words_in, part, part_in, zsum, sign_rank, sign_feat, right,
+    act_in, words_in, part, part_in, rank_sum, near_out, near_in, far_out, far_in,
+    sign_rank, sign_feat, right,
     raw, raw_in, mine, group, others, group_f, others_f,
-    act_send, act_recv, words_send, words_recv, part_send, part_recv, zsum_send, zsum_recv,
-    raw_send, raw_recv, group_send, group_recv, other_send, other_recv,
+    act_send, act_recv, words_send, words_recv, twin_send, twin_recv, part_send, part_recv,
+    near_send, near_recv, far_send, far_recv, raw_send, raw_recv,
+    group_send, group_recv, other_send, other_recv, word_y, word_z,
 ):
     my_dp = lax.axis_index("dp")
     me = lax.axis_index("mp")
@@ -70,6 +72,16 @@
     def arrived(ref, sem):
         return remote(ref, ref, sem, sem, my_dp, me)
 
+    half = my_dp % 2
+    twin = my_dp + 1 - 2 * half
+    near = z + 1 - 2 * (z % 2)
+    far = NZ - 1 - z
+    greeted = [(my_dp, to_x * NZ + z) for to_x in ring_x]
+    greeted += [(my_dp, x * NZ + near), (my_dp, x * NZ + far), (twin, me)]
+    barrier = pltpu.get_barrier_semaphore()
+    for to in greeted:
+        pl.semaphore_signal(barrier, inc=1, device_id=to, device_id_type=MESH)
+
     load_up = pltpu.make_async_copy(up_hbm, up, up_sem)
     load_grad = pltpu.make_async_copy(grad_hbm, grad, grad_sem)
     load_words = pltpu.make_async_copy(feat_words_hbm, feat_words, feat_words_sem)
@@ -79,11 +91,10 @@
     for load in (load_up, load_grad, load_words, load_act, load_rank_words, load_lengths):
         load.start()
 
-    barrier = pltpu.get_barrier_semaphore()
-    for to in mp_peers:
-        pl.semaphore_signal(barrier, inc=1, device_id=(my_dp, to), device_id_type=MESH)
-    for to in dp_peers:
-        pl.semaphore_signal(barrier, inc=1, device_id=(to, me), device_id_type=MESH)
+    @pl.when(z == 0)
+    def _():
+        for to in dp_peers:
+            pl.semaphore_signal(barrier, inc=1, device_id=(to, me), device_id_type=MESH)
 
     load_up.wait()
     load_grad.wait()
@@ -95,8 +106,17 @@
             .reshape(NZ, rows, LANES)
         )
     load_words.wait()
-    words_in[x] = feat_words[...].astype(jnp.int16)
-    pl.semaphore_wait(barrier, n_mp + n_dp - 2)
+    half_words = feat_words.shape[0] // 2
+    for at in range(2):
+        words_in[at, x] = feat_words[at * half_words:(at + 1) * half_words, :].astype(jnp.int16)
+
+    @pl.when(z == 0)
+    def _():
+        pl.semaphore_wait(barrier, len(greeted) + len(dp_peers))
+
+    @pl.when(z != 0)
+    def _():
+        pl.semaphore_wait(barrier, len(greeted))
 
     def send_part(to, piece):
         return remote(
@@ -106,7 +126,14 @@
 
     def send_words(to):
         return remote(
-            words_in.at[x], words_in.at[x], words_send.at[to], words_recv.at[x], my_dp, to * NZ + z
+            words_in.at[half, x], words_in.at[half, x],
+            words_send.at[to], words_recv.at[x], my_dp, to * NZ + z,
+        )
+
+    def send_twin(source):
+        return remote(
+            words_in.at[half, source], words_in.at[half, source],
+            twin_send.at[source], twin_recv.at[source], twin, me,
         )
 
     def send_act(to):
@@ -122,19 +149,29 @@
     for to in ring_x:
         send_act(to).start()
 
+    def unpack_slice(source):
+        for at in range(2):
+            sign_feat[at * sketch // 2:(at + 1) * sketch // 2, :] = unpack_signs(words_in[at, source])
+
     load_rank_words.wait()
     signs = unpack_signs(rank_words[...])
     sign_rank[...] = jnp.concatenate([signs, signs], axis=1)
-    sign_feat[...] = unpack_signs(words_in[x])
+    unpack_slice(x)
     load_act.wait()
     right[...] = lax.dot_general(
         act_in[x], sign_feat[...], NT, preferred_element_type=jnp.float32
     )
 
-    def send_zsum(to, piece):
-        return remote(
-            zsum.at[z, piece], zsum.at[z, piece],
-            zsum_send.at[to, piece], zsum_recv.at[z, piece], my_dp, x * NZ + to,
+    def send_near(piece):
+        return remote(
+            near_out.at[piece], near_in.at[piece],
+            near_send.at[piece], near_recv.at[piece], my_dp, x * NZ + near,
+        )
+
+    def send_far(piece):
+        return remote(
+            far_out.at[piece], far_in.at[piece],
+            far_send.at[piece], far_recv.at[piece], my_dp, x * NZ + far,
         )
 
     for piece in range(NZ):
@@ -142,13 +179,29 @@
         for source in ring_x:
             arrived(part_in.at[source, piece], part_recv.at[source, piece]).wait_recv()
             total = total + part_in[source, piece].astype(jnp.float32)
-        zsum[z, piece] = total.astype(jnp.bfloat16)
-        for to in ring_z:
-            send_zsum(to, piece).start()
+        rank_sum[piece] = total
+        near_out[piece] = total.astype(jnp.bfloat16)
+        send_near(piece).start()
+
+    for source in ring_x:
+        arrived(words_in.at[half, source], words_recv.at[source]).wait_recv()
+        send_twin(source).start()
+
+    for piece in range(NZ):
+        arrived(near_in.at[piece], near_recv.at[piece]).wait_recv()
+        total = rank_sum[piece] + near_in[piece].astype(jnp.float32)
+        rank_sum[piece] = total
+        far_out[piece] = total.astype(jnp.bfloat16)
+        send_far(piece).start()
+
+    @pl.when(z == 0)
+    def _():
+        for to in dp_peers:
+            pl.semaphore_signal(word_y, inc=1, device_id=(to, me), device_id_type=MESH)
 
     for source in ring_x[1:] + ring_x[:1]:
-        arrived(words_in.at[source], words_recv.at[source]).wait_recv()
-        sign_feat[...] = unpack_signs(words_in[source])
+        arrived(words_in.at[1 - half, source], twin_recv.at[source]).wait_recv()
+        unpack_slice(source)
         arrived(act_in.at[source], act_recv.at[source]).wait_recv()
         right[...] += lax.dot_general(
             act_in[source], sign_feat[...], NT, preferred_element_type=jnp.float32
@@ -163,10 +216,8 @@
         )
 
     for piece in range(NZ):
-        total = zsum[z, piece].astype(jnp.float32)
-        for source in ring_z:
-            arrived(zsum.at[source, piece], zsum_recv.at[source, piece]).wait_recv()
-            total = total + zsum[source, piece].astype(jnp.float32)
+        arrived(far_in.at[piece], far_recv.at[piece]).wait_recv()
+        total = rank_sum[piece] + far_in[piece].astype(jnp.float32)
         live = jnp.concatenate(
             [
                 (slot < lengths[x * examples + piece * own + example]).astype(jnp.float32)
@@ -193,6 +244,14 @@
         def _():
             send_raw(piece).start()
 
+    @pl.when(z == 0)
+    def _():
+        pl.semaphore_wait(word_y, len(dp_peers))
+        for to in ring_z:
+            pl.semaphore_signal(
+                word_z, inc=1, device_id=(my_dp, x * NZ + to), device_id_type=MESH
+            )
+
     raw_sum = raw[z]
     for source in ring_z:
         arrived(raw_in.at[source], raw_recv.at[source]).wait_recv()
@@ -201,6 +260,10 @@
         lines = raw_sum[example * blocks:(example + 1) * blocks, :]
         mean = jnp.sum(lines * lines, keepdims=True) / sketch
         mine[example * blocks:(example + 1) * blocks, :] = lines * lax.rsqrt(mean + 1e-06)
+    @pl.when(z != 0)
+    def _():
+        pl.semaphore_wait(word_z, 1)
+
     group[me] = mine[...].astype(jnp.bfloat16)
     others[my_dp] = mine[...].astype(jnp.bfloat16)
 
@@ -221,10 +284,12 @@
         for piece in range(NZ):
             send_part(to, piece).wait_send()
         send_words(to).wait_send()
+        send_twin(to).wait_send()
         send_act(to).wait_send()
+    for piece in range(NZ):
+        send_near(piece).wait_send()
+        send_far(piece).wait_send()
     for to in ring_z:
-        for piece in range(NZ):
-            send_zsum(to, piece).wait_send()
         send_raw(to).wait_send()
     remote(
         group.at[pl.ds(0, n_mp - 1)], group.at[pl.ds(0, n_mp - 1)], group_send, group_recv, my_dp, me
@@ -281,10 +346,14 @@
                 dma(()),
                 dma(()),
                 pltpu.VMEM((NX, quarter, features), bf16),
-                pltpu.VMEM((NX,) + feat_words.shape, jnp.int16),
+                pltpu.VMEM((2, NX, feat_words.shape[0] // 2, features), jnp.int16),
                 pltpu.VMEM(pieces, bf16),
                 pltpu.VMEM(pieces, bf16),
-                pltpu.VMEM((NZ,) + pieces[1:], bf16),
+                pltpu.VMEM(pieces[1:], f32),
+                pltpu.VMEM(pieces[1:], bf16),
+                pltpu.VMEM(pieces[1:], bf16),
+                pltpu.VMEM(pieces[1:], bf16),
+                pltpu.VMEM(pieces[1:], bf16),
                 pltpu.VMEM((sketch, 2 * rank), bf16),
                 pltpu.VMEM((sketch, features), bf16),
                 pltpu.VMEM((quarter, sketch), f32),
@@ -296,11 +365,11 @@
                 pltpu.VMEM((n_mp * width, LANES), f32),
                 pltpu.VMEM((n_dp * width, LANES), f32),
             ]
-            + [dma((NX,))] * 4
+            + [dma((NX,))] * 6
             + [dma((NX, NZ))] * 2
-            + [dma((NZ, NZ))] * 2
-            + [dma((NZ,))] * 2
-            + [dma(())] * 4,
+            + [dma((NZ,))] * 6
+            + [dma(())] * 4
+            + [pltpu.SemaphoreType.REGULAR] * 2,
             compiler_params=pltpu.CompilerParams(
                 collective_id=0, has_side_effects=True, vmem_limit_bytes=48 * 1024 * 1024
             ),

time: 41.7 us -> 40 us (0.959)
  Pallas kernels: 39.7 us -> 38 us
    pallas_call x1, Pallas kernels: 39.7 us -> 38 us  [per_device(): pl.pallas_call(functools.partial(kernel, n_dp, n_mp, seq), out_shape=[plt...]
where the time goes in v4:
time: 40 us; the launch traced here: 39.8 us
  Pallas kernels  38 us (95%)
  local copies, waits for them, and re-layouts  1.21 us (3%)
  between operations  0.64 us (2%)
    pallas_call x1, Pallas kernels, per_device(): pl.pallas_call(functools.partial(kernel, n_dp, n_mp, seq), out_shape=[plt...  38 us
    unnamed x2, local copies, waits for them, and re-layouts  1.21 us

profile of v4, /device:TPU:1, one launch (start us, length us, event | category | flops | bytes accessed | tf_op | source)
XLA Modules:
  0.0 39.8 jit_solution(1268023967635259027)
XLA Ops:
  0.6 38.0 %shard_map.77 = (bf16[2,1024]{1,0:T(2,128)(2,1)S(1)}, f32[32,2,32]{2,1,0:T(2,128)S(1)}) custom-call(bf16[1024,256]{1,0:T(8,128)(2,1)} %act_hbm.1, bf16[1024,256]{1,0:T(8,128)(2,1)} %grad_hbm.1, bf16[256,128]{1,0:T(8,128)(2,1)} %up_hbm.1, s32[64,128]{1,0:T(8,128)} %rank_words_hbm.1, s32[64,256]{1,0:T(8,128)} %feat_words_hbm.1, s32[32]{0:T(128)} %lengths_hbm.1), custom_call_target="tpu_custom_call" | custom-call | tf_op jit(solution)/shard_map/pallas_call | solution.py:329
  38.6 0.6 %copy.10 = bf16[2,1024]{1,0:T(2,128)(2,1)} copy(bf16[2,1024]{1,0:T(2,128)(2,1)S(1)} %get-tuple-element.6) | data formatting | bytes 8192
  39.2 0.6 %copy.11 = f32[32,32,2]{1,2,0:T(2,128)} copy(f32[32,32,2]{1,2,0:T(2,128)S(1)} %bitcast.1) | data formatting | bytes 16384

commit v5 on v4

--- a/solution.py
+++ b/solution.py
@@ -11,6 +11,7 @@
 NT = (((1,), (1,)), ((), ()))
 LANES = 128
 NX, NZ = 4, 4
+DIRECT = (0, NZ - 1)
 NY, NC = 8, 4
 
 
@@ -33,12 +34,12 @@
     sketch_out, cos_out,
     grad, up, rank_words, feat_words, lengths,
     up_sem, grad_sem, rank_words_sem, feat_words_sem, lengths_sem,
-    act_in, words_in, part, part_in, rank_sum, near_out, near_in, far_out, far_in,
+    act_own, act_own_sem, act_in, words_in, part, part_in, rank_sum, near_out, near_in, far_out, far_in, opposite_in,
     sign_rank, sign_feat, right,
     raw, raw_in, mine, group, others, group_f, others_f,
     act_send, act_recv, words_send, words_recv, twin_send, twin_recv, part_send, part_recv,
     near_send, near_recv, far_send, far_recv, raw_send, raw_recv,
-    group_send, group_recv, other_send, other_recv, word_y, word_z,
+    group_send, group_recv, other_send, other_recv, opposite_send, opposite_recv, word_near, word_y, word_z,
 ):
     my_dp = lax.axis_index("dp")
     me = lax.axis_index("mp")
@@ -48,7 +49,7 @@
     quarter = NZ * rows
     own = rows // seq
     examples = NZ * own
-    sketch = sign_feat.shape[0]
+    sketch = sign_feat.shape[1]
     blocks = sketch // LANES
     width = own * blocks
     ring_x = [(x + step) % NX for step in far_first(NX)]
@@ -85,7 +86,7 @@
     load_up = pltpu.make_async_copy(up_hbm, up, up_sem)
     load_grad = pltpu.make_async_copy(grad_hbm, grad, grad_sem)
     load_words = pltpu.make_async_copy(feat_words_hbm, feat_words, feat_words_sem)
-    load_act = pltpu.make_async_copy(rows_of(act_hbm, x), act_in.at[x], act_recv.at[x])
+    load_act = pltpu.make_async_copy(rows_of(act_hbm, x), act_own, act_own_sem)
     load_rank_words = pltpu.make_async_copy(rank_words_hbm, rank_words, rank_words_sem)
     load_lengths = pltpu.make_async_copy(lengths_hbm, lengths, lengths_sem)
     for load in (load_up, load_grad, load_words, load_act, load_rank_words, load_lengths):
@@ -136,30 +137,41 @@
             twin_send.at[source], twin_recv.at[source], twin, me,
         )
 
-    def send_act(to):
-        return remote(
-            rows_of(act_hbm, to), act_in.at[x], act_send.at[to], act_recv.at[x], my_dp, to * NZ + z
-        )
-
-    for piece in range(NZ):
+    def send_act(to, part_of):
+        first = pl.multiple_of(to * quarter + part_of * quarter // 2, quarter // 2)
+        return remote(
+            act_hbm.at[pl.ds(first, quarter // 2), :], act_in.at[x, part_of],
+            act_send.at[to, part_of], act_recv.at[x, part_of], my_dp, to * NZ + z,
+        )
+
+    for to in ring_x:
+        send_part(to, 0).start()
+    for to in ring_x:
+        send_words(to).start()
+    for piece in range(1, NZ):
         for to in ring_x:
             send_part(to, piece).start()
     for to in ring_x:
-        send_words(to).start()
-    for to in ring_x:
-        send_act(to).start()
+        send_act(to, 0).start()
+
+    pl.semaphore_signal(word_near, inc=1, device_id=(my_dp, x * NZ + near), device_id_type=MESH)
+    pl.semaphore_wait(word_near, 1)
+
+    @pl.when(z == 0)
+    def _():
+        for to in dp_peers:
+            pl.semaphore_signal(word_y, inc=1, device_id=(to, me), device_id_type=MESH)
 
     def unpack_slice(source):
         for at in range(2):
-            sign_feat[at * sketch // 2:(at + 1) * sketch // 2, :] = unpack_signs(words_in[at, source])
+            sign_feat[source, at * sketch // 2:(at + 1) * sketch // 2, :] = unpack_signs(words_in[at, source])
 
     load_rank_words.wait()
-    signs = unpack_signs(rank_words[...])
-    sign_rank[...] = jnp.concatenate([signs, signs], axis=1)
+    sign_rank[...] = unpack_signs(rank_words[...])
     unpack_slice(x)
     load_act.wait()
     right[...] = lax.dot_general(
-        act_in[x], sign_feat[...], NT, preferred_element_type=jnp.float32
+        act_own[...], sign_feat[x], NT, preferred_element_type=jnp.float32
     )
 
     def send_near(piece):
@@ -170,42 +182,59 @@
 
     def send_far(piece):
         return remote(
-            far_out.at[piece], far_in.at[piece],
+            (near_out if piece in DIRECT else far_out).at[piece], far_in.at[piece],
             far_send.at[piece], far_recv.at[piece], my_dp, x * NZ + far,
         )
 
-    for piece in range(NZ):
+    def send_opposite(piece):
+        return remote(
+            near_out.at[piece], opposite_in.at[piece],
+            opposite_send.at[piece], opposite_recv.at[piece], my_dp, x * NZ + (z + NZ // 2) % NZ,
+        )
+
+    def sum_row(piece):
         total = part[x, piece].astype(jnp.float32)
         for source in ring_x:
             arrived(part_in.at[source, piece], part_recv.at[source, piece]).wait_recv()
             total = total + part_in[source, piece].astype(jnp.float32)
         rank_sum[piece] = total
         near_out[piece] = total.astype(jnp.bfloat16)
+        if piece in DIRECT:
+            send_opposite(piece).start()
+            send_far(piece).start()
         send_near(piece).start()
-
+    def add_near(piece):
+        arrived(near_in.at[piece], near_recv.at[piece]).wait_recv()
+        total = rank_sum[piece] + near_in[piece].astype(jnp.float32)
+        rank_sum[piece] = total
+        if piece not in DIRECT:
+            far_out[piece] = total.astype(jnp.bfloat16)
+            send_far(piece).start()
+
+    def add_activations(part_of):
+        at = slice(part_of * quarter // 2, (part_of + 1) * quarter // 2)
+        right_sum = right[at, :]
+        for source in ring_x:
+            arrived(act_in.at[source, part_of], act_recv.at[source, part_of]).wait_recv()
+            right_sum = right_sum + lax.dot_general(
+                act_in[source, part_of], sign_feat[source], NT, preferred_element_type=jnp.float32
+            )
+        right[at, :] = right_sum
+
+    sum_row(0)
     for source in ring_x:
         arrived(words_in.at[half, source], words_recv.at[source]).wait_recv()
         send_twin(source).start()
-
-    for piece in range(NZ):
-        arrived(near_in.at[piece], near_recv.at[piece]).wait_recv()
-        total = rank_sum[piece] + near_in[piece].astype(jnp.float32)
-        rank_sum[piece] = total
-        far_out[piece] = total.astype(jnp.bfloat16)
-        send_far(piece).start()
-
-    @pl.when(z == 0)
-    def _():
-        for to in dp_peers:
-            pl.semaphore_signal(word_y, inc=1, device_id=(to, me), device_id_type=MESH)
-
-    for source in ring_x[1:] + ring_x[:1]:
+    sum_row(1)
+    for to in ring_x:
+        send_act(to, 1).start()
+    for source in ring_x:
         arrived(words_in.at[1 - half, source], twin_recv.at[source]).wait_recv()
         unpack_slice(source)
-        arrived(act_in.at[source], act_recv.at[source]).wait_recv()
-        right[...] += lax.dot_general(
-            act_in[source], sign_feat[...], NT, preferred_element_type=jnp.float32
-        )
+    sum_row(2)
+    sum_row(3)
+    add_near(1)
+    add_near(2)
 
     load_lengths.wait()
     slot = lax.broadcasted_iota(jnp.int32, (seq, LANES), 0)
@@ -216,8 +245,16 @@
         )
 
     for piece in range(NZ):
+        at = slice(piece * rows, (piece + 1) * rows)
+        if piece % (NZ // 2) == 0:
+            add_activations(piece // (NZ // 2))
+        if piece in DIRECT:
+            add_near(piece)
         arrived(far_in.at[piece], far_recv.at[piece]).wait_recv()
         total = rank_sum[piece] + far_in[piece].astype(jnp.float32)
+        if piece in DIRECT:
+            arrived(opposite_in.at[piece], opposite_recv.at[piece]).wait_recv()
+            total = total + opposite_in[piece].astype(jnp.float32)
         live = jnp.concatenate(
             [
                 (slot < lengths[x * examples + piece * own + example]).astype(jnp.float32)
@@ -227,11 +264,11 @@
         total = total * live
         high = total.astype(jnp.bfloat16)
         low = (total - high.astype(jnp.float32)).astype(jnp.bfloat16)
-        left = lax.dot_general(
-            jnp.concatenate([high, low], axis=1), sign_rank[...], NT,
-            preferred_element_type=jnp.float32,
-        )
-        product = left * right[piece * rows:(piece + 1) * rows, :]
+        pair = lax.dot_general(
+            jnp.concatenate([high, low]), sign_rank[...], NT, preferred_element_type=jnp.float32
+        )
+        left = pair[:rows] + pair[rows:]
+        product = left * right[at, :]
         sums = product.reshape(own, seq, sketch).sum(axis=1)
         for example in range(own):
             for block in range(blocks):
@@ -244,13 +281,15 @@
         def _():
             send_raw(piece).start()
 
-    @pl.when(z == 0)
-    def _():
-        pl.semaphore_wait(word_y, len(dp_peers))
-        for to in ring_z:
-            pl.semaphore_signal(
-                word_z, inc=1, device_id=(my_dp, x * NZ + to), device_id_type=MESH
-            )
+        if piece == 0:
+
+            @pl.when(z == 0)
+            def _():
+                pl.semaphore_wait(word_y, len(dp_peers))
+                for to in ring_z:
+                    pl.semaphore_signal(
+                        word_z, inc=1, device_id=(my_dp, x * NZ + to), device_id_type=MESH
+                    )
 
     raw_sum = raw[z]
     for source in ring_z:
@@ -285,7 +324,10 @@
             send_part(to, piece).wait_send()
         send_words(to).wait_send()
         send_twin(to).wait_send()
-        send_act(to).wait_send()
+        for part_of in range(2):
+            send_act(to, part_of).wait_send()
+    for piece in DIRECT:
+        send_opposite(piece).wait_send()
     for piece in range(NZ):
         send_near(piece).wait_send()
         send_far(piece).wait_send()
@@ -309,6 +351,17 @@
                 here, there.astype(jnp.bfloat16), NT, preferred_element_type=jnp.float32
             )
         cos_out[:, example, :] = cosines / sketch
+
+
+def hand_on(sketches, cosines, sketches_out, cosines_out, sketches_sem, cosines_sem):
+    copies = [
+        pltpu.make_async_copy(cosines, cosines_out, cosines_sem),
+        pltpu.make_async_copy(sketches, sketches_out, sketches_sem),
+    ]
+    for copy in copies:
+        copy.start()
+    for copy in copies:
+        copy.wait()
 
 
 def solution(mesh):
@@ -345,7 +398,9 @@
                 dma(()),
                 dma(()),
                 dma(()),
-                pltpu.VMEM((NX, quarter, features), bf16),
+                pltpu.VMEM((quarter, features), bf16),
+                dma(()),
+                pltpu.VMEM((NX, 2, quarter // 2, features), bf16),
                 pltpu.VMEM((2, NX, feat_words.shape[0] // 2, features), jnp.int16),
                 pltpu.VMEM(pieces, bf16),
                 pltpu.VMEM(pieces, bf16),
@@ -354,8 +409,9 @@
                 pltpu.VMEM(pieces[1:], bf16),
                 pltpu.VMEM(pieces[1:], bf16),
                 pltpu.VMEM(pieces[1:], bf16),
-                pltpu.VMEM((sketch, 2 * rank), bf16),
-                pltpu.VMEM((sketch, features), bf16),
+                pltpu.VMEM(pieces[1:], bf16),
+                pltpu.VMEM((sketch, rank), bf16),
+                pltpu.VMEM((NX, sketch, features), bf16),
                 pltpu.VMEM((quarter, sketch), f32),
                 pltpu.VMEM((NZ, width, LANES), f32),
                 pltpu.VMEM((NZ, width, LANES), f32),
@@ -365,15 +421,31 @@
                 pltpu.VMEM((n_mp * width, LANES), f32),
                 pltpu.VMEM((n_dp * width, LANES), f32),
             ]
-            + [dma((NX,))] * 6
+            + [dma((NX, 2))] * 2
+            + [dma((NX,))] * 4
             + [dma((NX, NZ))] * 2
             + [dma((NZ,))] * 6
             + [dma(())] * 4
-            + [pltpu.SemaphoreType.REGULAR] * 2,
+            + [dma((NZ,))] * 2
+            + [pltpu.SemaphoreType.REGULAR] * 3,
             compiler_params=pltpu.CompilerParams(
                 collective_id=0, has_side_effects=True, vmem_limit_bytes=48 * 1024 * 1024
             ),
         )(*[pltpu.with_memory_space_constraint(each, pltpu.HBM) for each in (activations, gradients, up_matrix, rank_words, feat_words, lengths)])
+        in_vmem = pl.BlockSpec(memory_space=pltpu.VMEM)
+        sketches, cosines = pl.pallas_call(
+            hand_on,
+            out_shape=[
+                jax.ShapeDtypeStruct(sketches.shape, bf16),
+                jax.ShapeDtypeStruct(cosines.shape, f32),
+            ],
+            in_specs=[in_vmem] * 2,
+            out_specs=[in_hbm] * 2,
+            scratch_shapes=[dma(()), dma(())],
+        )(
+            pltpu.with_memory_space_constraint(sketches, pltpu.VMEM),
+            pltpu.with_memory_space_constraint(cosines, pltpu.VMEM),
+        )
         return sketches, cosines.transpose(0, 2, 1)
 
     return jax.shard_map(

time: 40 us -> 38.5 us (0.963)
  local copies, waits for them, and re-layouts: 1.21 us -> 0 us
  Pallas kernels: 38 us -> 37.5 us
    unnamed x2 -> x0, local copies, waits for them, and re-layouts: 1.21 us -> none
    pallas_call x1, Pallas kernels: 38 us -> 36.8 us  [per_device(): pl.pallas_call(functools.partial(kernel, n_dp, n_mp, seq), out_shape=[plt...]
    pallas_call x0 -> x1, Pallas kernels: none -> 0.64 us  [per_device(): pl.pallas_call(hand_on, out_shape=[jax.ShapeDtypeStruct(sketches.shape, b...]
where the time goes in v5:
time: 38.5 us; the launch traced here: 38.1 us
  Pallas kernels  37.5 us (97%)
  between operations  0.64 us (2%)
    pallas_call x1, Pallas kernels, per_device(): pl.pallas_call(functools.partial(kernel, n_dp, n_mp, seq), out_shape=[plt...  36.8 us

profile of v5, /device:TPU:1, one launch (start us, length us, event | category | flops | bytes accessed | tf_op | source)
XLA Modules:
  0.0 38.1 jit_solution(11860275089781622010)
XLA Ops:
  0.6 36.8 %shard_map.77 = (bf16[2,1024]{1,0:T(2,128)(2,1)S(1)}, f32[32,2,32]{2,1,0:T(2,128)S(1)}) custom-call(bf16[1024,256]{1,0:T(8,128)(2,1)} %act_hbm.1, bf16[1024,256]{1,0:T(8,128)(2,1)} %grad_hbm.1, bf16[256,128]{1,0:T(8,128)(2,1)} %up_hbm.1, s32[64,128]{1,0:T(8,128)} %rank_words_hbm.1, s32[64,256]{1,0:T(8,128)} %feat_words_hbm.1, s32[32]{0:T(128)} %lengths_hbm.1), custom_call_target="tpu_custom_call" | custom-call | tf_op jit(solution)/shard_map/pallas_call | solution.py:382
  37.5 0.6 %shard_map.78 = (bf16[2,1024]{1,0:T(2,128)(2,1)}, f32[32,2,32]{2,1,0:T(2,128)}) custom-call(bf16[2,1024]{1,0:T(2,128)(2,1)S(1)} %get-tuple-element.6.sketches, f32[32,2,32]{2,1,0:T(2,128)S(1)} %get-tuple-element.7.cosines), custom_call_target="tpu_custom_call" | custom-call | tf_op jit(solution)/shard_map/pallas_call | solution.py:436

commit v6 on v5

--- a/solution.py
+++ b/solution.py
@@ -11,7 +11,6 @@
 NT = (((1,), (1,)), ((), ()))
 LANES = 128
 NX, NZ = 4, 4
-DIRECT = (0, NZ - 1)
 NY, NC = 8, 4
 
 
@@ -34,12 +33,12 @@
     sketch_out, cos_out,
     grad, up, rank_words, feat_words, lengths,
     up_sem, grad_sem, rank_words_sem, feat_words_sem, lengths_sem,
-    act_own, act_own_sem, act_in, words_in, part, part_in, rank_sum, near_out, near_in, far_out, far_in, opposite_in,
+    act_own, act_own_sem, act_in, words_in, part, part_in, rank_sum, rank_out, rank_in,
     sign_rank, sign_feat, right,
-    raw, raw_in, mine, group, others, group_f, others_f,
+    raw_in, mine, group, others, group_f, others_f,
     act_send, act_recv, words_send, words_recv, twin_send, twin_recv, part_send, part_recv,
-    near_send, near_recv, far_send, far_recv, raw_send, raw_recv,
-    group_send, group_recv, other_send, other_recv, opposite_send, opposite_recv, word_near, word_y, word_z,
+    rank_send, rank_recv, raw_send, raw_recv,
+    group_send, group_recv, other_send, other_recv, word_near, word_y, word_z,
 ):
     my_dp = lax.axis_index("dp")
     me = lax.axis_index("mp")
@@ -56,8 +55,6 @@
     ring_z = [(z + step) % NZ for step in far_first(NZ)]
     ring_y = [(y + step) % NY for step in far_first(NY)]
     ring_c = [(core + step) % NC for step in range(1, NC)]
-    mp_peers = [to_x * NZ + to_z for to_z in ring_z for to_x in ring_x + [x]]
-    mp_peers += [to_x * NZ + z for to_x in ring_x]
     dp_peers = [to_y * NC + to_c for to_y in ring_y for to_c in ring_c + [core]]
     dp_peers += [y * NC + to_c for to_c in ring_c]
 
@@ -151,16 +148,8 @@
     for piece in range(1, NZ):
         for to in ring_x:
             send_part(to, piece).start()
-    for to in ring_x:
-        send_act(to, 0).start()
 
     pl.semaphore_signal(word_near, inc=1, device_id=(my_dp, x * NZ + near), device_id_type=MESH)
-    pl.semaphore_wait(word_near, 1)
-
-    @pl.when(z == 0)
-    def _():
-        for to in dp_peers:
-            pl.semaphore_signal(word_y, inc=1, device_id=(to, me), device_id_type=MESH)
 
     def unpack_slice(source):
         for at in range(2):
@@ -174,22 +163,10 @@
         act_own[...], sign_feat[x], NT, preferred_element_type=jnp.float32
     )
 
-    def send_near(piece):
-        return remote(
-            near_out.at[piece], near_in.at[piece],
-            near_send.at[piece], near_recv.at[piece], my_dp, x * NZ + near,
-        )
-
-    def send_far(piece):
-        return remote(
-            (near_out if piece in DIRECT else far_out).at[piece], far_in.at[piece],
-            far_send.at[piece], far_recv.at[piece], my_dp, x * NZ + far,
-        )
-
-    def send_opposite(piece):
-        return remote(
-            near_out.at[piece], opposite_in.at[piece],
-            opposite_send.at[piece], opposite_recv.at[piece], my_dp, x * NZ + (z + NZ // 2) % NZ,
+    def send_rank(to, piece):
+        return remote(
+            rank_out.at[piece], rank_in.at[z, piece],
+            rank_send.at[to, piece], rank_recv.at[z, piece], my_dp, x * NZ + to,
         )
 
     def sum_row(piece):
@@ -198,18 +175,9 @@
             arrived(part_in.at[source, piece], part_recv.at[source, piece]).wait_recv()
             total = total + part_in[source, piece].astype(jnp.float32)
         rank_sum[piece] = total
-        near_out[piece] = total.astype(jnp.bfloat16)
-        if piece in DIRECT:
-            send_opposite(piece).start()
-            send_far(piece).start()
-        send_near(piece).start()
-    def add_near(piece):
-        arrived(near_in.at[piece], near_recv.at[piece]).wait_recv()
-        total = rank_sum[piece] + near_in[piece].astype(jnp.float32)
-        rank_sum[piece] = total
-        if piece not in DIRECT:
-            far_out[piece] = total.astype(jnp.bfloat16)
-            send_far(piece).start()
+        rank_out[piece] = total.astype(jnp.bfloat16)
+        for to in ring_z:
+            send_rank(to, piece).start()
 
     def add_activations(part_of):
         at = slice(part_of * quarter // 2, (part_of + 1) * quarter // 2)
@@ -221,7 +189,16 @@
             )
         right[at, :] = right_sum
 
+    pl.semaphore_wait(word_near, 1)
     sum_row(0)
+    for to in ring_x:
+        send_act(to, 0).start()
+
+    @pl.when(z == 0)
+    def _():
+        for to in dp_peers:
+            pl.semaphore_signal(word_y, inc=1, device_id=(to, me), device_id_type=MESH)
+
     for source in ring_x:
         arrived(words_in.at[half, source], words_recv.at[source]).wait_recv()
         send_twin(source).start()
@@ -233,28 +210,24 @@
         unpack_slice(source)
     sum_row(2)
     sum_row(3)
-    add_near(1)
-    add_near(2)
 
     load_lengths.wait()
     slot = lax.broadcasted_iota(jnp.int32, (seq, LANES), 0)
 
-    def send_raw(to):
-        return remote(
-            raw.at[to], raw_in.at[z], raw_send.at[to], raw_recv.at[z], my_dp, x * NZ + to
+    def send_raw(to, piece):
+        return remote(
+            raw_in.at[z, piece], raw_in.at[z, piece],
+            raw_send.at[to, piece], raw_recv.at[z, piece], my_dp, x * NZ + to,
         )
 
     for piece in range(NZ):
         at = slice(piece * rows, (piece + 1) * rows)
         if piece % (NZ // 2) == 0:
             add_activations(piece // (NZ // 2))
-        if piece in DIRECT:
-            add_near(piece)
-        arrived(far_in.at[piece], far_recv.at[piece]).wait_recv()
-        total = rank_sum[piece] + far_in[piece].astype(jnp.float32)
-        if piece in DIRECT:
-            arrived(opposite_in.at[piece], opposite_recv.at[piece]).wait_recv()
-            total = total + opposite_in[piece].astype(jnp.float32)
+        total = rank_sum[piece]
+        for source in ring_z:
+            arrived(rank_in.at[source, piece], rank_recv.at[source, piece]).wait_recv()
+            total = total + rank_in[source, piece].astype(jnp.float32)
         live = jnp.concatenate(
             [
                 (slot < lengths[x * examples + piece * own + example]).astype(jnp.float32)
@@ -273,13 +246,12 @@
         for example in range(own):
             for block in range(blocks):
                 line = example * blocks + block
-                raw[piece, line:line + 1, :] = sums[
+                raw_in[z, piece, line:line + 1, :] = sums[
                     example:example + 1, block * LANES:(block + 1) * LANES
                 ]
 
-        @pl.when(z != piece)
-        def _():
-            send_raw(piece).start()
+        for to in ring_z:
+            send_raw(to, piece).start()
 
         if piece == 0:
 
@@ -291,14 +263,21 @@
                         word_z, inc=1, device_id=(my_dp, x * NZ + to), device_id_type=MESH
                     )
 
-    raw_sum = raw[z]
-    for source in ring_z:
-        arrived(raw_in.at[source], raw_recv.at[source]).wait_recv()
-        raw_sum = raw_sum + raw_in[source]
-    for example in range(own):
-        lines = raw_sum[example * blocks:(example + 1) * blocks, :]
-        mean = jnp.sum(lines * lines, keepdims=True) / sketch
-        mine[example * blocks:(example + 1) * blocks, :] = lines * lax.rsqrt(mean + 1e-06)
+    def unit_sketches(owner):
+        for source in ring_z:
+            arrived(raw_in.at[source, owner], raw_recv.at[source, owner]).wait_recv()
+        total = raw_in[0, owner]
+        for source in range(1, NZ):
+            total = total + raw_in[source, owner]
+        units = []
+        for example in range(own):
+            lines = total[example * blocks:(example + 1) * blocks, :]
+            mean = jnp.sum(lines * lines, keepdims=True) / sketch
+            units.append(lines * lax.rsqrt(mean + 1e-06))
+        return jnp.concatenate(units)
+
+    mine[...] = unit_sketches(z)
+
     @pl.when(z != 0)
     def _():
         pl.semaphore_wait(word_z, 1)
@@ -306,14 +285,17 @@
     group[me] = mine[...].astype(jnp.bfloat16)
     others[my_dp] = mine[...].astype(jnp.bfloat16)
 
-    for at, to in enumerate(dp_peers):
+    for to in dp_peers:
         remote(
             others.at[my_dp], others.at[my_dp], other_send, other_recv, to, me
         ).start()
-        if at < len(mp_peers):
-            remote(
-                group.at[me], group.at[me], group_send, group_recv, my_dp, mp_peers[at]
-            ).start()
+    for owner in ring_z:
+        group[x * NZ + owner] = unit_sketches(owner).astype(jnp.bfloat16)
+    quarter_group = group.at[pl.ds(x * NZ, NZ)]
+    for to in ring_x:
+        remote(
+            quarter_group, quarter_group, group_send, group_recv, my_dp, to * NZ + z
+        ).start()
 
     sketch_out[...] = jnp.concatenate(
         [mine[pl.ds(block, own, stride=blocks), :] for block in range(blocks)], axis=1
@@ -326,15 +308,13 @@
         send_twin(to).wait_send()
         for part_of in range(2):
             send_act(to, part_of).wait_send()
-    for piece in DIRECT:
-        send_opposite(piece).wait_send()
-    for piece in range(NZ):
-        send_near(piece).wait_send()
-        send_far(piece).wait_send()
     for to in ring_z:
-        send_raw(to).wait_send()
+        for piece in range(NZ):
+            send_rank(to, piece).wait_send()
+            send_raw(to, piece).wait_send()
     remote(
-        group.at[pl.ds(0, n_mp - 1)], group.at[pl.ds(0, n_mp - 1)], group_send, group_recv, my_dp, me
+        group.at[pl.ds(0, n_mp - NZ)], group.at[pl.ds(0, n_mp - NZ)],
+        group_send, group_recv, my_dp, me,
     ).wait()
     group_f[...] = group[...].astype(jnp.float32).reshape(n_mp * width, LANES)
     remote(
@@ -406,15 +386,11 @@
                 pltpu.VMEM(pieces, bf16),
                 pltpu.VMEM(pieces[1:], f32),
                 pltpu.VMEM(pieces[1:], bf16),
-                pltpu.VMEM(pieces[1:], bf16),
-                pltpu.VMEM(pieces[1:], bf16),
-                pltpu.VMEM(pieces[1:], bf16),
-                pltpu.VMEM(pieces[1:], bf16),
+                pltpu.VMEM((NZ,) + pieces[1:], bf16),
                 pltpu.VMEM((sketch, rank), bf16),
                 pltpu.VMEM((NX, sketch, features), bf16),
                 pltpu.VMEM((quarter, sketch), f32),
-                pltpu.VMEM((NZ, width, LANES), f32),
-                pltpu.VMEM((NZ, width, LANES), f32),
+                pltpu.VMEM((NZ, NZ, width, LANES), f32),
                 pltpu.VMEM((width, LANES), f32),
                 pltpu.VMEM((n_mp, width, LANES), bf16),
                 pltpu.VMEM((n_dp, width, LANES), bf16),
@@ -424,9 +400,8 @@
             + [dma((NX, 2))] * 2
             + [dma((NX,))] * 4
             + [dma((NX, NZ))] * 2
-            + [dma((NZ,))] * 6
+            + [dma((NZ, NZ))] * 4
             + [dma(())] * 4
-            + [dma((NZ,))] * 2
             + [pltpu.SemaphoreType.REGULAR] * 3,
             compiler_params=pltpu.CompilerParams(
                 collective_id=0, has_side_effects=True, vmem_limit_bytes=48 * 1024 * 1024

time: 38.5 us -> 37.7 us (0.979)
  Pallas kernels: 37.5 us -> 37 us
    pallas_call x1, Pallas kernels: 36.8 us -> 36.3 us  [per_device(): pl.pallas_call(functools.partial(kernel, n_dp, n_mp, seq), out_shape=[plt...]
where the time goes in v6:
time: 37.7 us; the launch traced here: 37.6 us
  Pallas kernels  37 us (98%)
  between operations  0.64 us (2%)
    pallas_call x1, Pallas kernels, per_device(): pl.pallas_call(functools.partial(kernel, n_dp, n_mp, seq), out_shape=[plt...  36.3 us

profile of v6, /device:TPU:1, one launch (start us, length us, event | category | flops | bytes accessed | tf_op | source)
XLA Modules:
  0.0 37.6 jit_solution(6208974447088103345)
XLA Ops:
  0.6 36.3 %shard_map.77 = (bf16[2,1024]{1,0:T(2,128)(2,1)S(1)}, f32[32,2,32]{2,1,0:T(2,128)S(1)}) custom-call(bf16[1024,256]{1,0:T(8,128)(2,1)} %act_hbm.1, bf16[1024,256]{1,0:T(8,128)(2,1)} %grad_hbm.1, bf16[256,128]{1,0:T(8,128)(2,1)} %up_hbm.1, s32[64,128]{1,0:T(8,128)} %rank_words_hbm.1, s32[64,256]{1,0:T(8,128)} %feat_words_hbm.1, s32[32]{0:T(128)} %lengths_hbm.1), custom_call_target="tpu_custom_call" | custom-call | tf_op jit(solution)/shard_map/pallas_call | solution.py:362
  37.0 0.6 %shard_map.78 = (bf16[2,1024]{1,0:T(2,128)(2,1)}, f32[32,2,32]{2,1,0:T(2,128)}) custom-call(bf16[2,1024]{1,0:T(2,128)(2,1)S(1)} %get-tuple-element.6.sketches, f32[32,2,32]{2,1,0:T(2,128)S(1)} %get-tuple-element.7.cosines), custom_call_target="tpu_custom_call" | custom-call | tf_op jit(solution)/shard_map/pallas_call | solution.py:411

commit v7 on v6

--- a/solution.py
+++ b/solution.py
@@ -289,13 +289,15 @@
         remote(
             others.at[my_dp], others.at[my_dp], other_send, other_recv, to, me
         ).start()
-    for owner in ring_z:
+    def send_group(owner):
+        for to in ring_x:
+            ready = group.at[x * NZ + owner]
+            remote(ready, ready, group_send, group_recv, my_dp, to * NZ + z).start()
+
+    send_group(z)
+    for owner in [(z + step) % NZ for step in range(1, NZ)]:
         group[x * NZ + owner] = unit_sketches(owner).astype(jnp.bfloat16)
-    quarter_group = group.at[pl.ds(x * NZ, NZ)]
-    for to in ring_x:
-        remote(
-            quarter_group, quarter_group, group_send, group_recv, my_dp, to * NZ + z
-        ).start()
+        send_group(owner)
 
     sketch_out[...] = jnp.concatenate(
         [mine[pl.ds(block, own, stride=blocks), :] for block in range(blocks)], axis=1

time: 37.7 us -> 37.7 us (level)
  no operation moved by 1% of the time
where the time goes in v7:
time: 37.7 us; the launch traced here: 37.6 us
  Pallas kernels  37 us (98%)
  between operations  0.64 us (2%)
    pallas_call x1, Pallas kernels, per_device(): pl.pallas_call(functools.partial(kernel, n_dp, n_mp, seq), out_shape=[plt...  36.3 us

profile of v7, /device:TPU:1, one launch (start us, length us, event | category | flops | bytes accessed | tf_op | source)
XLA Modules:
  0.0 37.6 jit_solution(11660786645214887701)
XLA Ops:
  0.6 36.3 %shard_map.77 = (bf16[2,1024]{1,0:T(2,128)(2,1)S(1)}, f32[32,2,32]{2,1,0:T(2,128)S(1)}) custom-call(bf16[1024,256]{1,0:T(8,128)(2,1)} %act_hbm.1, bf16[1024,256]{1,0:T(8,128)(2,1)} %grad_hbm.1, bf16[256,128]{1,0:T(8,128)(2,1)} %up_hbm.1, s32[64,128]{1,0:T(8,128)} %rank_words_hbm.1, s32[64,256]{1,0:T(8,128)} %feat_words_hbm.1, s32[32]{0:T(128)} %lengths_hbm.1), custom_call_target="tpu_custom_call" | custom-call | tf_op jit(solution)/shard_map/pallas_call | solution.py:364
  37.0 0.6 %shard_map.78 = (bf16[2,1024]{1,0:T(2,128)(2,1)}, f32[32,2,32]{2,1,0:T(2,128)}) custom-call(bf16[2,1024]{1,0:T(2,128)(2,1)S(1)} %get-tuple-element.6.sketches, f32[32,2,32]{2,1,0:T(2,128)S(1)} %get-tuple-element.7.cosines), custom_call_target="tpu_custom_call" | custom-call | tf_op jit(solution)/shard_map/pallas_call | solution.py:413
